TPU v7x, 32 devices: a whole 2x2x4 slice. The times are simulated.
32 devices in a mesh: dp: 2 (over x), gx: 4 (over y, core), gy: 4 (over z).
Axes of the slice: x: 2, y: 2, z: 4, core: 2. Of those that a mesh axis runs over, the one named last changes fastest.
Arguments:
- tokens: bfloat16 [960, 11264], P('gy', ('dp', 'gx')), may hold values from -6 to 6
- segment_ids: int32 [8, 1408], P(('dp', 'gy')), may hold values from 0 to 3, never falling along the last dimension, each value on 1 to 704 neighbouring positions
- slot_table: int32 [5], replicated, may hold values from 0 to 7, as said below
- w_qkv: bfloat16 [960, 2560], P('gy', 'gx'), may hold values from -0.1875 to 0.1875
- w_out: bfloat16 [960, 1536], P('gy', 'gx'), may hold values from -1.5 to 1.5
- w_gate_up: bfloat16 [960, 2, 2560], P('gy', None, 'gx'), may hold values from -0.1875 to 0.1875
- w_down: bfloat16 [960, 2560], P('gy', 'gx'), may hold values from -0.125 to 0.125
- gain_attn: float32 [960], P('gy'), may hold values from 0.5 to 1.5
- gain_mlp: float32 [960], P('gy'), may hold values from 0.5 to 1.5
- cotangent: bfloat16 [960, 11264], P('gy', ('dp', 'gx')), may hold values from -6 to 6
Outputs:
- layer_out: bfloat16 [960, 11264], P('gy', ('dp', 'gx'))
- input_grad: bfloat16 [960, 11264], P('gy', ('dp', 'gx'))
- grad_qkv: float32 [960, 2560], P('gy', 'gx')
- grad_out: float32 [960, 1536], P('gy', 'gx')
- grad_gate_up: float32 [960, 2, 2560], P('gy', None, 'gx')
- grad_down: float32 [960, 2560], P('gy', 'gx')
- grad_gain_attn: float32 [960], P('gy')
- grad_gain_mlp: float32 [960], P('gy')
Inputs may be any that keep to these rules, and one draw needn't show every extreme that they name: `slot_table`: the 5 entries name distinct slots; slot // 2 is a weight-grid row. One row holds two groups in its slots 2 r and 2 r + 1, every other row one group in slot 2 r. `segment_ids`: within a sequence ids never fall.
All inputs are finite; a program needn't handle non-finite values.
Results may differ from a plain program's by a relative error of at most 0.019.
Values may be sent and summed in bfloat16 or wider, within the bound.
No kernel may reach another device: no remote copies, remote signals or barrier semaphores. Data moves between devices by JAX's collectives and lax.ppermute only.
A program may use at most 192 MiB of HBM per device.

v0:
```python
import jax
import jax.numpy as jnp
from jax import lax
from jax.sharding import PartitionSpec as P

D = 960
HD = 64
QPK = 3
L = 1408
SEGS = 4
BLOCK = 704


EPSILON = 1e-05
THETA_BASE = 100000.0
NEGATIVE = -1e30


def rope_angles(segment_row):
    doc_marks = (segment_row[:, None] == jnp.arange(SEGS, dtype=jnp.int32)[None, :]).astype(
        jnp.int32
    )
    counts = jnp.sum(doc_marks, axis=0)
    starts = jnp.cumsum(counts) - counts
    position = jnp.arange(L, dtype=jnp.int32) - jnp.sum(doc_marks * starts[None, :], axis=1)
    frequency = THETA_BASE ** (-2.0 * jnp.arange(HD // 2, dtype=jnp.float32) / HD)
    angles = position.astype(jnp.float32)[:, None] * frequency[None, :]
    return (jnp.cos(angles), jnp.sin(angles))


def rotate(values_in, cos_part, sin_part):
    half_width = values_in.shape[-1] // 2
    first_half = values_in[..., :half_width]
    second_half = values_in[..., half_width:]
    return jnp.concatenate(
        [
            first_half * cos_part - second_half * sin_part,
            second_half * cos_part + first_half * sin_part,
        ],
        axis=-1,
    )


def feature_sum(values_in):
    return lax.psum(values_in, "gy")


def grid_rows(values_in):
    return lax.all_gather(values_in, "gx", axis=1, tiled=True)


def block_rows(values_in):
    return lax.all_gather(values_in, "gy", axis=0, tiled=True)


def column_sum(term_fn, row_count):
    return lax.psum_scatter(
        term_fn(jnp.int32(0), lax.axis_size("gy") * row_count),
        "gy",
        scatter_dimension=0,
        tiled=True,
    )


def grid_sum(term_fn, row_count):
    return jnp.transpose(
        lax.psum_scatter(
            term_fn(jnp.int32(0), row_count * lax.axis_size("gx")).astype(jnp.bfloat16),
            "gx",
            scatter_dimension=0,
            tiled=True,
        ).astype(jnp.float32)
    )


def fold_block(pieces, step_fn, initial):
    return step_fn(initial, lax.all_gather(pieces, "gy", axis=0, tiled=True), jnp.int32(0))


def column_term(source):

    def column_row_term(first_row, row_count):
        return jnp.transpose(source)

    return column_row_term


def norm_forward(inputs, gain):
    squares = feature_sum(jnp.sum(inputs * inputs, axis=0))
    scale_rows = lax.rsqrt(squares / D + EPSILON)
    return (scale_rows, (inputs * scale_rows[None, :] * gain[:, None]).astype(jnp.bfloat16))


def norm_backward(inputs, scale_rows, gain, grad_normed):
    weighted = grad_normed * gain[:, None]
    inner = feature_sum(jnp.sum(weighted * inputs, axis=0))
    grad_gain = jnp.sum(grad_normed * inputs * scale_rows[None, :], axis=1)
    grad_in = scale_rows[None, :] * weighted - inputs * (scale_rows**3 * inner / D)[None, :]
    return (grad_in, grad_gain)


def block_scores(queries, key_rows, segment_row, first_row):
    query_rows = lax.dynamic_slice_in_dim(queries, first_row, BLOCK, 0)
    scores = jnp.einsum(
        "qhd,kd->hqk", query_rows, key_rows, preferred_element_type=jnp.float32
    ) * HD ** (-0.5)
    query_docs = lax.dynamic_slice_in_dim(segment_row, first_row, BLOCK, 0)
    query_index = first_row + jnp.arange(BLOCK, dtype=jnp.int32)
    allowed = (query_docs[:, None] == segment_row[None, :]) & (
        jnp.arange(L, dtype=jnp.int32)[None, :] <= query_index[:, None]
    )
    return (jnp.where(allowed[None], scores, NEGATIVE), query_rows)


def attend_forward(queries, key_rows, value_rows, segment_row):

    def one_block(block_index):
        masked, query_rows = block_scores(queries, key_rows, segment_row, block_index * BLOCK)
        row_peak = jnp.max(masked, axis=-1, keepdims=True)
        exp_scores = jnp.exp(masked - row_peak)
        row_total = jnp.sum(exp_scores, axis=-1, keepdims=True)
        weights_low = (exp_scores / row_total).astype(jnp.bfloat16)
        result = jnp.einsum(
            "hqk,kd->qhd", weights_low, value_rows, preferred_element_type=jnp.float32
        )
        return (result.astype(jnp.bfloat16), (row_peak + jnp.log(row_total))[..., 0])

    block_out, log_totals = lax.map(one_block, jnp.arange(L // BLOCK, dtype=jnp.int32))
    return (block_out.reshape(L, QPK, HD), log_totals)


def attend_backward(queries, key_rows, value_rows, segment_row, log_totals, grad_heads):
    scale_factor = HD ** (-0.5)

    def one_block(fold_state, block_index):
        grad_keys, grad_values = fold_state
        first_row = block_index * BLOCK
        masked, query_rows = block_scores(queries, key_rows, segment_row, first_row)
        weights_full = jnp.exp(masked - log_totals[block_index][..., None])
        grad_rows = lax.dynamic_slice_in_dim(grad_heads, first_row, BLOCK, 0)
        grad_weights = jnp.einsum(
            "qhd,kd->hqk", grad_rows, value_rows, preferred_element_type=jnp.float32
        )
        inner = jnp.sum(weights_full * grad_weights, axis=-1, keepdims=True)
        grad_scores = (weights_full * (grad_weights - inner)).astype(jnp.bfloat16)
        grad_query = (
            jnp.einsum("hqk,kd->qhd", grad_scores, key_rows, preferred_element_type=jnp.float32)
            * scale_factor
        )
        grad_keys = (
            grad_keys
            + jnp.einsum("hqk,qhd->kd", grad_scores, query_rows, preferred_element_type=jnp.float32)
            * scale_factor
        )
        grad_values = grad_values + jnp.einsum(
            "hqk,qhd->kd",
            weights_full.astype(jnp.bfloat16),
            grad_rows,
            preferred_element_type=jnp.float32,
        )
        return ((grad_keys, grad_values), grad_query)

    empty_rows = jnp.zeros((L, HD), jnp.float32)
    (grad_keys, grad_values), grad_query = lax.scan(
        one_block, (empty_rows, empty_rows), jnp.arange(L // BLOCK, dtype=jnp.int32)
    )
    return (grad_query.reshape(L, QPK, HD), grad_keys, grad_values)


def to_pairs(values_in, seq_local):
    shaped = values_in.reshape((seq_local, L) + values_in.shape[1:])
    moved = jnp.swapaxes(shaped, 1, 2)
    return moved.reshape((-1, L) + values_in.shape[2:])


def from_pairs(values_in, seq_local, slot_count):
    shaped = values_in.reshape((seq_local, slot_count, L) + values_in.shape[2:])
    moved = jnp.swapaxes(shaped, 1, 2)
    return moved.reshape((seq_local * L, slot_count) + values_in.shape[2:])


def per_device(
    tokens, segment_ids, slot_table, w_qkv, w_out, w_gate_up, w_down, gain_attn, gain_mlp, cotangent
):
    feature_count = tokens.shape[0]
    grid_count = tokens.shape[1]
    seq_local = segment_ids.shape[0]
    block_count = seq_local * L
    slot_width = (QPK + 2) * HD
    slot_count = w_qkv.shape[1] // slot_width
    group_rows = grid_count * lax.axis_size("gx")
    slot_ids = lax.axis_index("gx") * slot_count + jnp.arange(slot_count, dtype=jnp.int32)
    live_flags = jnp.any(slot_table[None, :] == slot_ids[:, None], axis=1)
    live_scale = live_flags.astype(jnp.float32)
    query_width = QPK * HD

    def feature_project(source, form, weight_local):

        def feature_row_term(first_row, row_count):
            return jnp.einsum(form, source, weight_local, preferred_element_type=jnp.float32)

        return column_sum(feature_row_term, block_count)

    inputs = tokens.astype(jnp.float32)
    scale_one, normed_one = norm_forward(inputs, gain_attn)
    full_one = grid_rows(normed_one)
    projected = feature_project(full_one, "dt,de->te", w_qkv).reshape(
        block_count, slot_count, slot_width
    )
    cos_part, sin_part = jax.vmap(rope_angles)(segment_ids)
    cos_part = cos_part.reshape(block_count, HD // 2)
    sin_part = sin_part.reshape(block_count, HD // 2)
    queries = projected[:, :, :query_width].reshape(block_count, slot_count, QPK, HD)
    queries = rotate(queries, cos_part[:, None, None, :], sin_part[:, None, None, :]).astype(
        jnp.bfloat16
    )
    key_rows = rotate(
        projected[:, :, query_width : query_width + HD], cos_part[:, None, :], sin_part[:, None, :]
    ).astype(jnp.bfloat16)
    value_rows = projected[:, :, query_width + HD :].astype(jnp.bfloat16)
    query_pairs = to_pairs(queries, seq_local)
    key_pairs = to_pairs(key_rows, seq_local)
    value_pairs = to_pairs(value_rows, seq_local)
    segment_pairs = jnp.repeat(segment_ids, slot_count, axis=0)
    live_pairs = jnp.tile(live_flags, seq_local)

    def pair_forward(pair_item):
        query_one, key_one, value_one, segment_one, live_one = pair_item
        return attend_forward(query_one, key_one, value_one, segment_one)

    head_pairs, log_totals = lax.map(
        pair_forward, (query_pairs, key_pairs, value_pairs, segment_pairs, live_pairs)
    )
    head_out = (
        from_pairs(head_pairs, seq_local, slot_count)
        * live_scale.astype(jnp.bfloat16)[None, :, None, None]
    )
    head_flat = head_out.reshape(block_count, slot_count * query_width)
    heads_full = block_rows(head_flat)

    def out_term(first_row, row_count):
        return jnp.einsum("te,de->td", heads_full, w_out, preferred_element_type=jnp.float32)

    attention = grid_sum(out_term, grid_count)
    middle = inputs + attention
    scale_two, normed_two = norm_forward(middle, gain_mlp)
    full_two = grid_rows(normed_two)
    gate_up = feature_project(full_two, "dt,dkf->tkf", w_gate_up)
    gate_part = gate_up[:, 0]
    up_part = gate_up[:, 1]
    sigma = jax.nn.sigmoid(gate_part)
    hidden = (gate_part * sigma * up_part).astype(jnp.bfloat16)
    hidden_full = block_rows(hidden)

    def down_term(first_row, row_count):
        return jnp.einsum("tf,df->td", hidden_full, w_down, preferred_element_type=jnp.float32)

    mlp_out = grid_sum(down_term, grid_count)
    layer_out = (middle + mlp_out).astype(jnp.bfloat16)
    grad_full = grid_rows(cotangent)
    grad_down = jnp.einsum("dt,tf->df", grad_full, hidden_full, preferred_element_type=jnp.float32)
    grad_hidden = feature_project(grad_full, "dt,df->tf", w_down)
    grad_gate = grad_hidden * up_part * sigma * (1.0 + gate_part * (1.0 - sigma))
    grad_up = grad_hidden * gate_part * sigma
    grad_pair = jnp.stack([grad_gate, grad_up], axis=1).astype(jnp.bfloat16)

    def gate_fold(fold_state, shard_piece, first_row):
        weight_acc = jnp.einsum(
            "dt,tkf->dkf", full_two, shard_piece, preferred_element_type=jnp.float32
        )
        rows_acc = jnp.einsum(
            "tkf,dkf->dt", shard_piece, w_gate_up, preferred_element_type=jnp.float32
        )
        return (weight_acc, rows_acc)

    grad_gate_up, normed_two_part = fold_block(
        grad_pair,
        gate_fold,
        (
            jnp.zeros(w_gate_up.shape, jnp.float32),
            jnp.zeros((feature_count, group_rows), jnp.float32),
        ),
    )
    grad_normed_two = grid_sum(column_term(normed_two_part), grid_count)
    grad_middle_norm, grad_gain_mlp = norm_backward(middle, scale_two, gain_mlp, grad_normed_two)
    grad_middle = cotangent.astype(jnp.float32) + grad_middle_norm
    grad_attention = grad_middle.astype(jnp.bfloat16)
    grad_att_full = grid_rows(grad_attention)
    grad_out = jnp.einsum(
        "dt,te->de", grad_att_full, heads_full, preferred_element_type=jnp.float32
    )
    grad_heads = feature_project(grad_att_full, "dt,de->te", w_out).astype(jnp.bfloat16)
    grad_head_pairs = to_pairs(grad_heads.reshape(block_count, slot_count, QPK, HD), seq_local)

    def pair_backward(pair_item):
        query_one, key_one, value_one, segment_one, totals_one, grad_one, live_one = pair_item
        return attend_backward(query_one, key_one, value_one, segment_one, totals_one, grad_one)

    grad_q_pairs, grad_k_pairs, grad_v_pairs = lax.map(
        pair_backward,
        (
            query_pairs,
            key_pairs,
            value_pairs,
            segment_pairs,
            log_totals,
            grad_head_pairs,
            live_pairs,
        ),
    )
    grad_queries = from_pairs(grad_q_pairs, seq_local, slot_count)
    grad_keys = from_pairs(grad_k_pairs, seq_local, slot_count)
    grad_values = from_pairs(grad_v_pairs, seq_local, slot_count)
    grad_queries = rotate(grad_queries, cos_part[:, None, None, :], -sin_part[:, None, None, :])
    grad_keys = rotate(grad_keys, cos_part[:, None, :], -sin_part[:, None, :])
    grad_projected = jnp.concatenate(
        [grad_queries.reshape(block_count, slot_count, query_width), grad_keys, grad_values],
        axis=-1,
    )
    grad_projected = (
        (grad_projected * live_scale[None, :, None])
        .astype(jnp.bfloat16)
        .reshape(block_count, slot_count * slot_width)
    )

    def qkv_fold(fold_state, shard_piece, first_row):
        weight_acc = jnp.einsum(
            "dt,te->de", full_one, shard_piece, preferred_element_type=jnp.float32
        )
        rows_acc = jnp.einsum("te,de->dt", shard_piece, w_qkv, preferred_element_type=jnp.float32)
        return (weight_acc, rows_acc)

    grad_qkv, normed_one_part = fold_block(
        grad_projected,
        qkv_fold,
        (jnp.zeros(w_qkv.shape, jnp.float32), jnp.zeros((feature_count, group_rows), jnp.float32)),
    )
    grad_normed_one = grid_sum(column_term(normed_one_part), grid_count)
    grad_input_norm, grad_gain_attn = norm_backward(inputs, scale_one, gain_attn, grad_normed_one)
    input_grad = (grad_middle + grad_input_norm).astype(jnp.bfloat16)
    grad_qkv, grad_out, grad_gate_up, grad_down = (
        lax.psum(grad_qkv.astype(jnp.bfloat16), "dp").astype(jnp.float32),
        lax.psum(grad_out.astype(jnp.bfloat16), "dp").astype(jnp.float32),
        lax.psum(grad_gate_up.astype(jnp.bfloat16), "dp").astype(jnp.float32),
        lax.psum(grad_down.astype(jnp.bfloat16), "dp").astype(jnp.float32),
    )
    grad_gain_attn, grad_gain_mlp = lax.psum((grad_gain_attn, grad_gain_mlp), ("dp", "gx"))
    return (
        layer_out,
        input_grad,
        grad_qkv,
        grad_out,
        grad_gate_up,
        grad_down,
        grad_gain_attn,
        grad_gain_mlp,
    )


def solution(mesh):
    placed = (
        P("gy", ("dp", "gx")),
        P(("dp", "gy"), None),
        P(),
        P("gy", "gx"),
        P("gy", "gx"),
        P("gy", None, "gx"),
        P("gy", "gx"),
        P("gy"),
        P("gy"),
        P("gy", ("dp", "gx")),
    )
    return jax.shard_map(
        per_device,
        mesh=mesh,
        in_specs=placed,
        out_specs=(
            P("gy", ("dp", "gx")),
            P("gy", ("dp", "gx")),
            P("gy", "gx"),
            P("gy", "gx"),
            P("gy", None, "gx"),
            P("gy", "gx"),
            P("gy"),
            P("gy"),
        ),
        check_vma=False,
    )
```

profile of v0, /device:TPU:0, one launch (start us, length us, event | category | flops | bytes accessed | tf_op | source)
XLA Modules:
  0.0 2260.0 jit_solution(6478352829592330480)
XLA Ops:
  8.6 13.7 psum.70
  25.1 24.3 %all-gather.9.cloned.1.call-done = bf16[240,5632]{1,0:T(8,128)(2,1)} async-done(((bf16[240,1408]{1,0:T(8,128)(2,1)}), bf16[240,5632]{1,0:T(8,128)(2,1)}) %all-gather.9.cloned.1.call-update) | async-done | bytes 2703376 | tf_op jit(solution)/shard_map/all_gather | solution.py:49
  49.5 9.4 fusion.87
  62.8 237.7 %reduce-scatter.17.cloned.1.call-done = f32[1408,640]{1,0:T(8,128)} async-done(((f32[5632,640]{1,0:T(8,128)}), f32[1408,640]{1,0:T(8,128)}) %reduce-scatter.17.cloned.1.call-update) | async-done | bytes 3604496 | tf_op jit(solution)/shard_map/reduce_scatter | solution.py:57
  312.6 104.9 %while.54 = (s32[]{:T(128)}, bf16[2,1408,3,64]{1,3,2,0:T(8,128)(2,1)}, f32[2,2,3,704]{3,2,1,0:T(4,128)}, bf16[2,1408,3,64]{1,3,2,0:T(8,128)(2,1)}, bf16[2,1408,6...) while((s32[]{:T(128)}, ...), condition=%wide.region_11.12_spmd, body=%wide.region_6.11_spmd.sunk | while | flops 800057984 | bytes 45805524 | solution.py:231
  314.8 45.8 %while.57 = (s32[]{:T(128)}, bf16[2,704,3,64]{1,3,2,0:T(8,128)(2,1)S(1)}, f32[2,3,704]{2,1,0:T(4,128)S(1)}, s32[2]{0:T(128)S(1)}, s32[1408]{0:T(1024)S(1)}, /*in...) while((s32[]{:T(128)}, ...), condition=%wide.region_10.10_spmd, body=%wide.region_7.9_spmd.sunk | while | flops 800057984 | bytes 40706252 | solution.py:128
  317.1 6.9 bitcast_reduce_fusion.2
  324.0 6.5 fusion.148
  330.5 7.2 fusion.149
  340.0 6.9 bitcast_reduce_fusion.2
  346.9 6.5 fusion.148
  353.4 7.2 fusion.149
  367.2 45.8 %while.57 = (s32[]{:T(128)}, bf16[2,704,3,64]{1,3,2,0:T(8,128)(2,1)S(1)}, f32[2,3,704]{2,1,0:T(4,128)S(1)}, s32[2]{0:T(128)S(1)}, s32[1408]{0:T(1024)S(1)}, /*in...) while((s32[]{:T(128)}, ...), condition=%wide.region_10.10_spmd, body=%wide.region_7.9_spmd.sunk | while | flops 800057984 | bytes 40706252 | solution.py:128
  369.6 6.9 bitcast_reduce_fusion.2
  376.4 6.5 fusion.148
  382.9 7.2 fusion.149
  392.5 6.9 bitcast_reduce_fusion.2
  399.4 6.5 fusion.148
  405.9 7.2 fusion.149
  420.0 84.1 %all-gather.11.cloned.1.call-done = bf16[5632,384]{0,1:T(8,128)(2,1)} async-done(((bf16[1408,384]{0,1:T(8,128)(2,1)}), bf16[5632,384]{0,1:T(8,128)(2,1)}) %all-gather.11.cloned.1.call-update) | async-done | bytes 4325392 | tf_op jit(solution)/shard_map/all_gather | solution.py:53
  511.3 34.4 %reduce-scatter.25.cloned.1.call-done = bf16[1408,240]{1,0:T(8,128)(2,1)} async-done(((bf16[5632,240]{1,0:T(8,128)(2,1)}), bf16[1408,240]{1,0:T(8,128)(2,1)}) %reduce-scatter.25.cloned.1.call-update) | async-done | bytes 675856
  547.4 12.3 psum.71
  560.9 12.3 all-gather.17.cloned.1.call-done
  573.2 9.5 fusion.88
  582.8 18.5 all-gather.13.cloned.1.call-done
  601.4 14.7 fusion.47
  616.1 229.2 %reduce-scatter.21.cloned.1.call-done = f32[1408,640]{1,0:T(8,128)} async-done(((f32[5632,640]{1,0:T(8,128)}), f32[1408,640]{1,0:T(8,128)}) %reduce-scatter.21.cloned.1.call-update) | async-done | bytes 3604496 | tf_op jit(solution)/shard_map/reduce_scatter | solution.py:57
  845.4 476.8 %reduce-scatter.19.cloned.1.call-done = f32[1408,2,640]{2,0,1:T(8,128)} async-done(((f32[5632,2,640]{2,0,1:T(8,128)}), f32[1408,2,640]{2,0,1:T(8,128)}) %reduce-scatter.19.cloned.1.call-update) | async-done | bytes 7208976 | tf_op jit(solution)/shard_map/reduce_scatter | solution.py:57
  1322.1 6.1 fusion.50
  1330.4 250.4 %all-gather.19.cloned.1.call-done = bf16[5632,2,640]{2,0,1:T(8,128)(2,1)} async-done(((bf16[1408,2,640]{2,0,1:T(8,128)(2,1)}), bf16[5632,2,640]{2,0,1:T(8,128)(2,1)}) %all-gather.19.cloned.1.call-update) | async-done | bytes 14417936 | tf_op jit(solution)/shard_map/all_gather | solution.py:77
  1580.8 15.4 fusion.43
  1600.8 34.6 %reduce-scatter.29.cloned.1.call-done = bf16[1408,240]{1,0:T(8,128)(2,1)} async-done(((bf16[5632,240]{1,0:T(8,128)(2,1)}), bf16[1408,240]{1,0:T(8,128)(2,1)}) %reduce-scatter.29.cloned.1.call-update) | async-done | bytes 675856
  1638.0 11.8 psum.72
  1651.8 23.4 %all-gather.21.cloned.1.call-done = bf16[240,5632]{1,0:T(8,128)(2,1)} async-done(((bf16[240,1408]{1,0:T(8,128)(2,1)}), bf16[240,5632]{1,0:T(8,128)(2,1)}) %all-gather.21.cloned.1.call-update) | async-done | bytes 2703376 | tf_op jit(solution)/shard_map/all_gather | solution.py:49
  1675.2 6.8 fusion.89
  1683.7 147.1 %reduce-scatter.23.cloned.1.call-done = f32[1408,384]{1,0:T(8,128)} async-done(((f32[5632,384]{1,0:T(8,128)}), f32[1408,384]{1,0:T(8,128)}) %reduce-scatter.23.cloned.1.call-update) | async-done | bytes 2162704 | tf_op jit(solution)/shard_map/reduce_scatter | solution.py:57
  1834.5 120.2 %while.56 = (s32[]{:T(128)}, f32[2,1408,3,64]{1,3,2,0:T(8,128)}, f32[2,1408,64]{1,2,0:T(8,128)}, f32[2,1408,64]{1,2,0:T(8,128)}, bf16[2,1408,3,64]{1,3,2,0:T(8,1...) while((s32[]{:T(128)}, f32[2,1408,3,64]{1,3,2,0:T(8,128)}, ...), condition=%wide.region_27.28_spmd, body=%wide.region_23.27_spmd.sunk | while | flops 1933486720 | bytes 126862760 | solution.py:299
  1839.1 44.1 %while.58 = (s32[]{:T(128)}, f32[1408,64]{0,1:T(8,128)}, f32[1408,64]{0,1:T(8,128)}, f32[2,704,3,64]{1,3,2,0:T(8,128)}, s32[2]{0:T(128)S(1)}, /*index=5*/s32[140...) while((s32[]{:T(128)}, f32[1408,64]{0,1:T(8,128)}, ...), condition=%wide.region_26.26_spmd.clone, body=%wide.region_24.25_spmd.clone.sunk | while | flops 1933486720 | bytes 115913776 | solution.py:164
  1899.1 44.1 %while.58 = (s32[]{:T(128)}, f32[1408,64]{0,1:T(8,128)}, f32[1408,64]{0,1:T(8,128)}, f32[2,704,3,64]{1,3,2,0:T(8,128)}, s32[2]{0:T(128)S(1)}, /*index=5*/s32[140...) while((s32[]{:T(128)}, f32[1408,64]{0,1:T(8,128)}, ...), condition=%wide.region_26.26_spmd.clone, body=%wide.region_24.25_spmd.clone.sunk | while | flops 1933486720 | bytes 115913776 | solution.py:164
  1971.9 7.8 fusion.72
  1979.6 8.2 fusion.69
  1990.2 103.5 %all-gather.23.cloned.1.call-done = bf16[5632,640]{0,1:T(8,128)(2,1)} async-done(((bf16[1408,640]{0,1:T(8,128)(2,1)}), bf16[5632,640]{0,1:T(8,128)(2,1)}) %all-gather.23.cloned.1.call-update) | async-done | bytes 7208976 | tf_op jit(solution)/shard_map/all_gather | solution.py:77
  2093.7 6.1 convolution_convert_fusion.4
  2109.0 21.6 reduce-scatter.27.cloned.1.call-done
  2132.8 49.5 %all-reduce.4.cloned.1.call-done = (bf16[240,2,640]{2,0,1:T(8,128)(2,1)}, bf16[240,640]{1,0:T(8,128)(2,1)}, bf16[240,384]{1,0:T(8,128)(2,1)}, bf16[240,640]{1,0:T(8,128)(2,1)}) async-done(((bf16[240,2,640]{2,0,1:T(8,128)(2,1)}, bf16[240,640]{1,0:T(8,128)(2,1)}, bf16[240,384]{1,0:T(8,128)(2,1)}, bf16[240,640]{1,0:T(8,128)(2,1)}), (bf16[240,2,640]{2,0,1:T(8,128)(2,1)}, bf16[240,640]{1,0:T(8,128)(2,1)}, ...) | async-done | bytes 1413136 | tf_op jit(solution)/shard_map/psum | solution.py:344
  2189.5 31.9 %reduce-scatter.31.cloned.1.call-done = bf16[1408,240]{1,0:T(8,128)(2,1)} async-done(((bf16[5632,240]{1,0:T(8,128)(2,1)}), bf16[1408,240]{1,0:T(8,128)(2,1)}) %reduce-scatter.31.cloned.1.call-update) | async-done | bytes 675856
  2225.4 11.8 psum.73
  2237.3 12.5 all-reduce
  (377 shorter events, 223.8 us)
Async XLA Ops:
  7.2 594.2 %copy-start = (bf16[240,2,640]{2,1,0:T(2,128)(2,1)S(1)}, bf16[240,2,640]{2,1,0:T(2,128)(2,1)}, u32[]{:S(2)}) copy-start(bf16[240,2,640]{2,1,0:T(2,128)(2,1)} %param.23) | copy-start | bytes 1843204
  7.2 42.3 %copy-start.32 = (bf16[240,640]{1,0:T(8,128)(2,1)S(1)}, bf16[240,640]{1,0:T(8,128)(2,1)}, u32[]{:S(2)}) copy-start(bf16[240,640]{1,0:T(8,128)(2,1)} %param.21) | copy-start | bytes 921604
  7.2 42.3 %all-gather.9.cloned.1.call-start = ((), (), s32[]{:S(2)}) async-start(), calls=%async_computation.8 | async-start | bytes 3379200 | tf_op jit(solution)/shard_map/all_gather | solution.py:49
  22.3 36.6 %copy-start.41 = (f32[1408]{0:T(1024)}, f32[1408]{0:T(1024)S(1)}, u32[]{:S(2)}) copy-start(f32[1408]{0:T(1024)S(1)} %psum.70) | copy-start | bytes 16900
  25.1 275.5 %reduce-scatter.17.cloned.1.call-start = ((), (), s32[]{:S(2)}) async-start(), calls=%async_computation.9 | async-start | bytes 18022400 | tf_op jit(solution)/shard_map/reduce_scatter | solution.py:57
  58.9 445.2 %all-gather.11.cloned.1.call-start = ((), (), s32[]{:S(2)}) async-start(), calls=%async_computation.10 | async-start | bytes 5406720 | tf_op jit(solution)/shard_map/all_gather | solution.py:53
  62.8 247.6 %copy-start.20 = (f32[1408,32]{0,1:T(8,128)}, f32[1408,32]{0,1:T(8,128)S(1)}, u32[]{:S(2)}) copy-start(f32[1408,32]{0,1:T(8,128)S(1)} %get-tuple-element.399) | copy-start | bytes 540676
  312.6 105.0 %copy-start.48 = (bf16[384]{0:T(512)(128)(2,1)S(1)}, bf16[384]{0:T(512)(128)(2,1)}, u32[]{:S(2)}) copy-start(bf16[384]{0:T(512)(128)(2,1)} %mul.374) | copy-start | bytes 2308
  417.5 86.6 %copy-start.25 = (bf16[240,384]{1,0:T(8,128)(2,1)S(1)}, bf16[240,384]{1,0:T(8,128)(2,1)}, u32[]{:S(2)}) copy-start(bf16[240,384]{1,0:T(8,128)(2,1)} %param.22) | copy-start | bytes 552964
  420.0 125.7 %reduce-scatter.25.cloned.1.call-start = ((), (), s32[]{:S(2)}) async-start(), calls=%async_computation.20 | async-start | bytes 3604480
  510.7 36.5 %copy-start.9 = (bf16[240,1408]{1,0:T(8,128)(2,1)S(1)}, bf16[240,1408]{1,0:T(8,128)(2,1)}, u32[]{:S(2)}) copy-start(bf16[240,1408]{1,0:T(8,128)(2,1)} %param.18) | copy-start | bytes 2027524
  510.7 49.0 %copy-start.43 = (f32[240]{0:T(256)S(1)}, f32[240]{0:T(256)}, u32[]{:S(2)}) copy-start(f32[240]{0:T(256)} %param.26) | copy-start | bytes 2884
  510.7 62.6 %all-gather.17.cloned.1.call-start = ((), (), s32[]{:S(2)}) async-start(), calls=%async_computation.14 | async-start | bytes 3379200 | tf_op jit(solution)/shard_map/all_gather | solution.py:49
  511.3 62.0 %copy-start.30 = (bf16[240,640]{1,0:T(8,128)(2,1)S(1)}, bf16[240,640]{1,0:T(8,128)(2,1)}, u32[]{:S(2)}) copy-start(bf16[240,640]{1,0:T(8,128)(2,1)} %param.24) | copy-start | bytes 921604
  511.3 90.1 %all-gather.13.cloned.1.call-start = ((), (), s32[]{:S(2)}) async-start(), calls=%async_computation.11 | async-start | bytes 3379200 | tf_op jit(solution)/shard_map/all_gather | solution.py:49
  547.1 1102.7 %copy-start.13 = (bf16[1408,240]{0,1:T(8,128)(2,1)}, bf16[1408,240]{0,1:T(8,128)(2,1)S(1)}, u32[]{:S(2)}) copy-start(bf16[1408,240]{0,1:T(8,128)(2,1)S(1)} %copy.64) | copy-start | bytes 2027524
  559.7 1090.1 %copy-start.35 = (f32[1408]{0:T(1024)}, f32[1408]{0:T(1024)S(1)}, u32[]{:S(2)}) copy-start(f32[1408]{0:T(1024)S(1)} %add_rsqrt_fusion) | copy-start | bytes 16900
  560.9 284.5 %reduce-scatter.21.cloned.1.call-start = ((), (), s32[]{:S(2)}) async-start(), calls=%async_computation.15 | async-start | bytes 18022400 | tf_op jit(solution)/shard_map/reduce_scatter | solution.py:57
  582.8 739.3 %reduce-scatter.19.cloned.1.call-start = ((), (), s32[]{:S(2)}) async-start(), calls=%async_computation.12 | async-start | bytes 36044800 | tf_op jit(solution)/shard_map/reduce_scatter | solution.py:57
  616.1 964.7 %all-gather.19.cloned.1.call-start = ((), (), s32[]{:S(2)}) async-start(), calls=%async_computation.16 | async-start | bytes 18022400 | tf_op jit(solution)/shard_map/all_gather | solution.py:77
  1330.4 305.1 %reduce-scatter.29.cloned.1.call-start = ((), (), s32[]{:S(2)}) async-start(), calls=%async_computation.22 | async-start | bytes 3604480
  1600.7 49.7 %copy-start.18 = (bf16[240,1408]{1,0:T(8,128)(2,1)S(1)}, bf16[240,1408]{1,0:T(8,128)(2,1)}, u32[]{:S(2)}) copy-start(bf16[240,1408]{1,0:T(8,128)(2,1)} %param.27) | copy-start | bytes 2027524
  1600.8 74.4 %all-gather.21.cloned.1.call-start = ((), (), s32[]{:S(2)}) async-start(), calls=%async_computation.17 | async-start | bytes 3379200 | tf_op jit(solution)/shard_map/all_gather | solution.py:49
  1636.9 14.9 copy-start.15
  1651.8 179.0 %reduce-scatter.23.cloned.1.call-start = ((), (), s32[]{:S(2)}) async-start(), calls=%async_computation.18 | async-start | bytes 10813440 | tf_op jit(solution)/shard_map/reduce_scatter | solution.py:57
  1682.0 281.5 %all-gather.15.cloned.1.call-start = ((), (), s32[]{:S(2)}) async-start(), calls=%async_computation.13 | async-start | bytes 9011200 | tf_op jit(solution)/shard_map/all_gather | solution.py:53
  1683.4 410.2 %all-gather.23.cloned.1.call-start = ((), (), s32[]{:S(2)}) async-start(), calls=%async_computation.19 | async-start | bytes 9011200 | tf_op jit(solution)/shard_map/all_gather | solution.py:77
  1960.4 170.2 %reduce-scatter.27.cloned.1.call-start = ((), (), s32[]{:S(2)}) async-start(), calls=%async_computation.21 | async-start | bytes 3604480
  1971.8 7.8 copy-start.17
  1971.8 210.5 %all-reduce.4.cloned.1.call-start = ((), (), s32[]{:S(2)}) async-start(), calls=%async_computation.24 | async-start | bytes 2826240 | tf_op jit(solution)/shard_map/psum | solution.py:344
  1971.9 16.0 slice-start
  1979.6 8.2 slice-start.1
  1979.6 8.2 copy-start.22
  1987.9 105.8 %copy-start.23 = (bf16[240,5632]{1,0:T(8,128)(2,1)S(1)}, bf16[240,5632]{1,0:T(8,128)(2,1)}, u32[]{:S(2)}) copy-start(bf16[240,5632]{1,0:T(8,128)(2,1)} %all-gather.9.cloned.1.call-done) | copy-start | bytes 8110084
  1990.2 109.7 %copy-start.33 = (bf16[240,640]{1,0:T(8,128)(2,1)S(1)}, bf16[240,640]{1,0:T(8,128)(2,1)}, u32[]{:S(2)}) copy-start(bf16[240,640]{1,0:T(8,128)(2,1)} %param.21) | copy-start | bytes 921604
  2099.8 121.6 %reduce-scatter.31.cloned.1.call-start = ((), (), s32[]{:S(2)}) async-start(), calls=%async_computation.23 | async-start | bytes 3604480
  2182.3 41.4 %copy-start.10 = (bf16[240,1408]{1,0:T(8,128)(2,1)S(1)}, bf16[240,1408]{1,0:T(8,128)(2,1)}, u32[]{:S(2)}) copy-start(bf16[240,1408]{1,0:T(8,128)(2,1)} %param.18) | copy-start | bytes 2027524
  2182.3 41.4 %copy-start.38 = (f32[1408]{0:T(1024)S(1)}, f32[1408]{0:T(1024)}, u32[]{:S(2)}) copy-start(f32[1408]{0:T(1024)} %copy-done.37) | copy-start | bytes 16900
  2182.3 41.4 %copy-start.46 = (f32[240]{0:T(256)S(1)}, f32[240]{0:T(256)}, u32[]{:S(2)}) copy-start(f32[240]{0:T(256)} %param.25) | copy-start | bytes 2884
  2186.6 50.6 %copy-start.42 = (f32[1408]{0:T(1024)S(1)}, f32[1408]{0:T(1024)}, u32[]{:S(2)}) copy-start(f32[1408]{0:T(1024)} %copy-done.41) | copy-start | bytes 16900
  2186.6 50.6 %copy-start.49 = (f32[240]{0:T(256)S(1)}, f32[240]{0:T(256)}, u32[]{:S(2)}) copy-start(f32[240]{0:T(256)} %get-tuple-element.292) | copy-start | bytes 2884
  2186.6 63.2 %copy-start.14 = (bf16[1408,240]{0,1:T(8,128)(2,1)S(1)}, bf16[1408,240]{0,1:T(8,128)(2,1)}, u32[]{:S(2)}) copy-start(bf16[1408,240]{0,1:T(8,128)(2,1)} %copy-done.13) | copy-start | bytes 2027524
  2186.6 63.2 %copy-start.16 = (bf16[1408,240]{0,1:T(8,128)(2,1)S(1)}, bf16[1408,240]{0,1:T(8,128)(2,1)}, u32[]{:S(2)}) copy-start(bf16[1408,240]{0,1:T(8,128)(2,1)} %copy-done.15) | copy-start | bytes 2027524
  2186.6 63.2 %copy-start.19 = (bf16[240,1408]{1,0:T(8,128)(2,1)S(1)}, bf16[240,1408]{1,0:T(8,128)(2,1)}, u32[]{:S(2)}) copy-start(bf16[240,1408]{1,0:T(8,128)(2,1)} %param.27) | copy-start | bytes 2027524
  2186.6 63.1 %copy-start.36 = (f32[1408]{0:T(1024)S(1)}, f32[1408]{0:T(1024)}, u32[]{:S(2)}) copy-start(f32[1408]{0:T(1024)} %copy-done.35) | copy-start | bytes 16900
  2186.6 63.1 %copy-start.40 = (f32[1408]{0:T(1024)S(1)}, f32[1408]{0:T(1024)}, u32[]{:S(2)}) copy-start(f32[1408]{0:T(1024)} %copy-done.39) | copy-start | bytes 16900
  2186.7 63.1 %copy-start.44 = (f32[240]{0:T(256)S(1)}, f32[240]{0:T(256)}, u32[]{:S(2)}) copy-start(f32[240]{0:T(256)} %param.26) | copy-start | bytes 2884
  2237.3 15.9 copy-start.1
  (52 other events, 116.6 us)
Sparse Core Ops, SparseCore 0:
  25.2 24.2 all-gather.8
  59.0 241.4 reduce-scatter.16
  420.1 83.9 all-gather.10
  510.8 34.8 reduce-scatter.24
  547.2 26.0 all-gather.16
  575.3 26.0 all-gather.12
  603.8 241.4 reduce-scatter.20
  847.9 474.2 reduce-scatter.18
  1330.5 250.2 all-gather.18
  1600.9 34.5 reduce-scatter.28
  1651.9 23.2 all-gather.20
  1682.2 148.5 reduce-scatter.22
  1832.4 131.1 all-gather.14
  1965.0 128.5 all-gather.22
  2096.0 34.5 reduce-scatter.26
  2133.7 48.5 all-reduce.3
  2184.8 36.5 reduce-scatter.30
where the time goes:
time: 2270 us; the launch traced here: 2260 us
  waiting for transfers between devices  1780 us (78%)
  matrix products  206 us (9%)
  local copies, waits for them, and re-layouts  97.1 us (4%)
  other arithmetic  82.1 us (4%)
  blocking collectives  62.1 us (3%)
    reduce_scatter x4, waiting for transfers between devices, column_sum(): lax.psum_scatter(term_fn(jnp.int32(0), lax.axis_size('gy') * row_count),...  1090 us
    all_gather x2, waiting for transfers between devices, fold_block(): lax.all_gather(pieces, 'gy', axis=0, tiled=True)  354 us
    unnamed x21, waiting for transfers between devices  123 us
    all_gather x2, waiting for transfers between devices, block_rows(): return lax.all_gather(values_in, 'gy', axis=0, tiled=True)  87.2 us
    all_gather x4, waiting for transfers between devices, grid_rows(): return lax.all_gather(values_in, 'gx', axis=1, tiled=True)  78.6 us
    dot_general x8, matrix products, block_scores(): jnp.einsum('qhd,kd->hqk', query_rows, key_rows, preferred_element_type=jn...  51.4 us
    psum x4, blocking collectives, feature_sum(): return lax.psum(values_in, 'gy')  49.6 us
    psum x1, waiting for transfers between devices, per_device(): lax.psum(grad_gate_up.astype(jnp.bfloat16), 'dp').astype(jnp.float32)  49.5 us
  transfers between devices with their start and end apart: 17, of which 17 were waited for; matrix products, arithmetic and copies ran while one was open for 9% of the time, Pallas kernels for 0%

commit v1 on v0

v1 whole, which is shorter than its diff:
```python
import functools

import jax
import jax.numpy as jnp
from jax import lax
from jax.experimental import pallas as pl
from jax.experimental.pallas import tpu as pltpu
from jax.sharding import PartitionSpec as P

D = 960
HD = 64
QPK = 3
L = 1408
SEGS = 4
QW = QPK * HD
SLOT_W = QW + 2 * HD
PACK = SLOT_W + QW
GROUPS = 5
ROWS = 4
CH = L // ROWS
FB = D // ROWS
ODD = PACK // ROWS

EPSILON = 1e-05
THETA_BASE = 100000.0
NEGATIVE = -1e30
SEQ_MAP = (0, 2, 1, 3)
SEQ_BACK = (0, 2, 1, 3)
BF = jnp.bfloat16
F32 = jnp.float32
VMEM_LIMIT = 40 * 1024 * 1024


def tn(a, b):
    return lax.dot_general(a, b, (((0,), (0,)), ((), ())), preferred_element_type=F32)


def nn(a, b):
    return lax.dot_general(a, b, (((1,), (0,)), ((), ())), preferred_element_type=F32)


def nt(a, b):
    return lax.dot_general(a, b, (((1,), (1,)), ((), ())), preferred_element_type=F32)


def qkv_kernel(x_ref, gain_ref, cos_ref, sin_ref, w_ref, qs_ref, kv_ref, n1_ref, r1_ref):
    @pl.when(pl.program_id(0) == 0)
    def _():
        x = x_ref[...].astype(F32)
        r1 = lax.rsqrt(jnp.sum(x * x, axis=0, keepdims=True) / D + EPSILON)
        r1_ref[...] = r1
        n1_ref[...] = (x * r1 * gain_ref[...]).astype(BF)

    p = tn(w_ref[0, :, :SLOT_W], n1_ref[...])
    cos_a = cos_ref[...]
    sin_a = sin_ref[...]
    half = HD // 2
    for j in range(QPK + 1):
        a = p[j * HD : j * HD + half]
        b = p[j * HD + half : (j + 1) * HD]
        first = (a * cos_a - b * sin_a).astype(BF)
        second = (b * cos_a + a * sin_a).astype(BF)
        if j < QPK:
            first = (first.astype(F32) * HD**-0.5).astype(BF)
            second = (second.astype(F32) * HD**-0.5).astype(BF)
            qs_ref[0, j * HD : j * HD + half] = first
            qs_ref[0, j * HD + half : (j + 1) * HD] = second
        else:
            kv_ref[0, :half] = first
            kv_ref[0, half:HD] = second
    kv_ref[0, HD:] = p[(QPK + 1) * HD :].astype(BF)


def attend_kernel(
    flags, qs_ref, kv0, kv1, kv2, kv3, bias_ref, w_ref, x_ref, gain_ref,
    o_ref, lse_ref, h_ref, n2_ref, r2_ref, m_s, l_s, acc_s,
):
    g = pl.program_id(0)
    kvs = (kv0, kv1, kv2, kv3)

    def fold(k, fresh):
        keys = kvs[k][0, :HD]
        values = kvs[k][0, HD:]
        bias = bias_ref[k]
        for j in range(QPK):
            s = tn(keys, qs_ref[0, j * HD : (j + 1) * HD]) + bias
            top = jnp.max(s, axis=0, keepdims=True)
            if fresh:
                m = top
                e = jnp.exp(s - m)
                l_s[j : j + 1] = jnp.sum(e, axis=0, keepdims=True)
                acc_s[j * HD : (j + 1) * HD] = nn(values, e.astype(BF))
            else:
                old = m_s[j : j + 1]
                m = jnp.maximum(old, top)
                fade = jnp.exp(old - m)
                e = jnp.exp(s - m)
                l_s[j : j + 1] = l_s[j : j + 1] * fade + jnp.sum(e, axis=0, keepdims=True)
                acc_s[j * HD : (j + 1) * HD] = acc_s[j * HD : (j + 1) * HD] * fade + nn(
                    values, e.astype(BF)
                )
            m_s[j : j + 1] = m

    fold(0, True)
    for k in range(1, ROWS):
        pl.when(flags[k] != 0)(functools.partial(fold, k, False))
    for j in range(QPK):
        total = l_s[j : j + 1]
        o_ref[0, j * HD : (j + 1) * HD] = (acc_s[j * HD : (j + 1) * HD] / total).astype(BF)
        lse_ref[0, j : j + 1] = m_s[j : j + 1] + jnp.log(total)
    part = nn(w_ref[0, :, SLOT_W:], o_ref[0])

    @pl.when(g == 0)
    def _():
        h_ref[...] = x_ref[...].astype(F32) + part

    @pl.when(g != 0)
    def _():
        h_ref[...] += part

    @pl.when(g == GROUPS - 1)
    def _():
        h = h_ref[...]
        r2 = lax.rsqrt(jnp.sum(h * h, axis=0, keepdims=True) / D + EPSILON)
        r2_ref[...] = r2
        n2_ref[...] = (h * r2 * gain_ref[...]).astype(BF)


def attend_back_kernel(
    flags, qs_ref, kv0, kv1, kv2, kv3, bias_ref, w_ref, o_ref, lse_ref, datt_ref, cos_ref, sin_ref,
    dq_ref, d0, d1, d2, d3, do_s, dl_s, dq_s,
):
    kvs = (kv0, kv1, kv2, kv3)
    outs = (d0, d1, d2, d3)
    do_s[...] = tn(w_ref[0, :, SLOT_W:], datt_ref[...]).astype(BF)
    for j in range(QPK):
        rows = slice(j * HD, (j + 1) * HD)
        dl_s[j : j + 1] = jnp.sum(
            do_s[rows].astype(F32) * o_ref[0, rows].astype(F32), axis=0, keepdims=True
        )

    def fold(k, fresh):
        keys = kvs[k][0, :HD]
        values = kvs[k][0, HD:]
        bias = bias_ref[k]
        dk = jnp.zeros((HD, CH), F32)
        dv = jnp.zeros((HD, CH), F32)
        for j in range(QPK):
            rows = slice(j * HD, (j + 1) * HD)
            s = tn(keys, qs_ref[0, rows]) + bias
            p = jnp.exp(s - lse_ref[0, j : j + 1])
            do_j = do_s[rows]
            dp = tn(values, do_j)
            ds = (p * (dp - dl_s[j : j + 1])).astype(BF)
            dv = dv + nt(do_j, p.astype(BF))
            dk = dk + nt(qs_ref[0, rows], ds)
            dq = nn(keys, ds)
            if fresh:
                dq_s[rows] = dq
            else:
                dq_s[rows] += dq
        outs[k][0, :HD] = dk.astype(outs[k].dtype)
        outs[k][0, HD:] = dv.astype(outs[k].dtype)

    fold(0, True)
    for k in range(1, ROWS):
        pl.when(flags[k] != 0)(functools.partial(fold, k, False))

        @pl.when(flags[k] == 0)
        def _(k=k):
            outs[k][...] = jnp.zeros(outs[k].shape, outs[k].dtype)

    cos_a = cos_ref[...]
    sin_a = sin_ref[...]
    half = HD // 2
    for j in range(QPK):
        a = dq_s[j * HD : j * HD + half] * HD**-0.5
        b = dq_s[j * HD + half : (j + 1) * HD] * HD**-0.5
        dq_ref[0, j * HD : j * HD + half] = (a * cos_a + b * sin_a).astype(BF)
        dq_ref[0, j * HD + half : (j + 1) * HD] = (b * cos_a - a * sin_a).astype(BF)


def mlp_kernel(wg, wu, wd, *refs):
    count = len(refs) // 7
    for i in range(count):
        n2 = refs[i]
        dy = refs[count + i]
        a_ref, dg_ref, du_ref, mlp_ref, dn_ref = refs[2 * count + 5 * i : 2 * count + 5 * i + 5]
        width = wg.shape[1]
        step = 128
        for f in range(0, width, step):
            cols = slice(f, f + step)
            gate = tn(wg[:, cols], n2[...])
            up = tn(wu[:, cols], n2[...])
            da = tn(wd[:, cols], dy[...])
            sigma = jax.nn.sigmoid(gate)
            silu = gate * sigma
            a_ref[cols] = (silu * up).astype(BF)
            dg_ref[cols] = (da * up * sigma * (1.0 + gate * (1.0 - sigma))).astype(BF)
            du_ref[cols] = (da * silu).astype(BF)
        dn_ref[...] = (nn(wg[...], dg_ref[...]) + nn(wu[...], du_ref[...])).astype(BF)
        mlp_ref[...] = nn(wd[...], a_ref[...]).astype(BF)


def whole(shape):
    return pl.BlockSpec(shape, lambda *_: (0,) * len(shape))


def per_group(*shape):
    return pl.BlockSpec((1,) + shape, lambda g, *_: (g, 0, 0))


def kv_blocks():
    def spec(k):
        return pl.BlockSpec(
            (1, 2 * HD, CH), lambda g, *_: (jnp.where(g < ROWS, g ^ k, g), 0, 0)
        )

    return [spec(k) for k in range(ROWS)]


def params():
    return pltpu.CompilerParams(vmem_limit_bytes=VMEM_LIMIT)


def sds(shape, dtype):
    return jax.ShapeDtypeStruct(shape, dtype)


def call_qkv(x, gain, cos_a, sin_a, w5):
    return pl.pallas_call(
        qkv_kernel,
        grid=(GROUPS,),
        in_specs=[whole((D, CH)), whole((D, 1)), whole((HD // 2, CH)), whole((HD // 2, CH)), per_group(D, PACK)],
        out_specs=[per_group(QW, CH), per_group(2 * HD, CH), whole((D, CH)), whole((1, CH))],
        out_shape=[
            sds((GROUPS, QW, CH), BF), sds((GROUPS, 2 * HD, CH), BF), sds((D, CH), BF), sds((1, CH), F32),
        ],
        compiler_params=params(),
        name="qkv",
    )(x, gain, cos_a, sin_a, w5)


def call_attend(flags, qs, kvs, bias, w5, x, gain):
    return pl.pallas_call(
        attend_kernel,
        grid_spec=pltpu.PrefetchScalarGridSpec(
            num_scalar_prefetch=1,
            grid=(GROUPS,),
            in_specs=[per_group(QW, CH)] + kv_blocks()
            + [whole((ROWS, CH, CH)), per_group(D, PACK), whole((D, CH)), whole((D, 1))],
            out_specs=[per_group(QW, CH), per_group(8, CH), whole((D, CH)), whole((D, CH)), whole((1, CH))],
            scratch_shapes=[pltpu.VMEM((8, CH), F32), pltpu.VMEM((8, CH), F32), pltpu.VMEM((QW, CH), F32)],
        ),
        out_shape=[
            sds((GROUPS, QW, CH), BF), sds((GROUPS, 8, CH), F32), sds((D, CH), F32), sds((D, CH), BF),
            sds((1, CH), F32),
        ],
        compiler_params=params(),
        name="attend",
    )(flags, qs, *kvs, bias, w5, x, gain)


def call_attend_back(flags, qs, kvs, bias, w5, o, lse, datt, cos_a, sin_a):
    return pl.pallas_call(
        attend_back_kernel,
        grid_spec=pltpu.PrefetchScalarGridSpec(
            num_scalar_prefetch=1,
            grid=(GROUPS,),
            in_specs=[per_group(QW, CH)] + kv_blocks()
            + [whole((ROWS, CH, CH)), per_group(D, PACK), per_group(QW, CH), per_group(8, CH),
               whole((D, CH)), whole((HD // 2, CH)), whole((HD // 2, CH))],
            out_specs=[per_group(QW, CH)] + kv_blocks(),
            scratch_shapes=[pltpu.VMEM((QW, CH), BF), pltpu.VMEM((8, CH), F32), pltpu.VMEM((QW, CH), F32)],
        ),
        out_shape=[sds((GROUPS, QW, CH), BF), sds((GROUPS, 2 * HD, CH), F32)]
        + [sds((GROUPS, 2 * HD, CH), BF)] * 3,
        compiler_params=params(),
        name="attend_back",
    )(flags, qs, *kvs, bias, w5, o, lse, datt, cos_a, sin_a)


def call_mlp(wg, wu, wd, n2s, dys):
    width = wg.shape[1]
    count = len(n2s)
    outs = pl.pallas_call(
        mlp_kernel,
        out_shape=[sds((width, CH), BF), sds((width, CH), BF), sds((width, CH), BF), sds((D, CH), BF), sds((D, CH), BF)]
        * count,
        compiler_params=params(),
        name="mlp",
    )(wg, wu, wd, *n2s, *dys)
    return [outs[5 * i : 5 * i + 5] for i in range(count)]


def swap(values, bit):
    return lax.ppermute(values, "gx", [(i, i ^ bit) for i in range(ROWS)])


def row_gather(own):
    mate = swap(own, 1)
    far = swap(own, 2)
    return own, mate, far, swap(far, 1)


def add(a, b):
    return (a.astype(F32) + b.astype(F32)).astype(BF)


def row_scatter(blocks):
    far = add(blocks[2], swap(blocks[3], 1))
    near = blocks[0].astype(F32) + swap(blocks[1], 1).astype(F32)
    return near + swap(far, 2).astype(F32)


def ring(values):
    return lax.ppermute(values, "gy", [(i, (i + 1) % ROWS) for i in range(ROWS)])


def ring_scatter(take, iy):
    moving = take((iy + 3) % ROWS).astype(BF)
    for s in range(ROWS - 1):
        moving = ring(moving).astype(F32) + take((iy + 2 - s) % ROWS).astype(F32)
        if s < ROWS - 2:
            moving = moving.astype(BF)
    return moving


def dp_sum(values):
    if lax.axis_size("dp") == 2:
        return values.astype(F32) + lax.ppermute(values, "dp", [(0, 1), (1, 0)]).astype(F32)
    return lax.psum(values, "dp").astype(F32)


def to_tokens(values, ix, iy):
    parts = jnp.transpose(values.reshape(FB, ROWS, CH), (1, 0, 2))
    out = jnp.zeros((D, CH), values.dtype)
    for k in range(ROWS):
        pairs = [(a * ROWS + b, (b ^ k) * ROWS + SEQ_MAP[a]) for a in range(ROWS) for b in range(ROWS)]
        piece = lax.ppermute(lax.dynamic_index_in_dim(parts, iy ^ k, 0, keepdims=False), ("gx", "gy"), pairs)
        out = lax.dynamic_update_slice(out, piece, (FB * (ix ^ k), 0))
    return out


def to_features(values, ix, iy):
    out = jnp.zeros((ROWS, FB, CH), values.dtype)
    for k in range(ROWS):
        pairs = [(a * ROWS + b, SEQ_BACK[b] * ROWS + (a ^ k)) for a in range(ROWS) for b in range(ROWS)]
        piece = lax.ppermute(
            lax.dynamic_slice(values, (FB * (ix ^ k), 0), (FB, CH)), ("gx", "gy"), pairs
        )
        out = lax.dynamic_update_slice(out, piece[None], (iy ^ k, 0, 0))
    return jnp.transpose(out, (1, 0, 2)).reshape(FB, L)


def gather_attention_weights(w_qkv, w_out, odd_row, ix, iy):
    even = jnp.concatenate([w_qkv[:, :SLOT_W], w_out[:, :QW]], axis=1)
    odd = jnp.concatenate([w_qkv[:, SLOT_W:], w_out[:, QW:]], axis=1)
    odd = jnp.where(ix == odd_row, odd, jnp.zeros_like(odd))
    quarters = [lax.dynamic_slice(odd, (0, ODD * (ix ^ k)), (FB, ODD)) for k in range(ROWS)]
    quarter = row_scatter(quarters).astype(BF)
    moving = jnp.concatenate([even, quarter], axis=1)
    w5 = jnp.zeros((GROUPS, D, PACK), BF)
    for j in range(ROWS):
        if j:
            moving = ring(moving)
        at = FB * ((iy - j) % ROWS)
        for k, piece in enumerate(row_gather(moving)):
            w5 = lax.dynamic_update_slice(w5, piece[None, :, :PACK], (k, at, 0))
            w5 = lax.dynamic_update_slice(w5, piece[None, :, PACK:], (GROUPS - 1, at, ODD * (ix ^ k)))
    return w5


def gather_mlp_weights(packed, iy):
    width = packed.shape[1]
    full = jnp.zeros((D, width), BF)
    if lax.axis_size("dp") == 2:
        part = (width // 2 + 127) // 128 * 128
        at_own = lax.axis_index("dp") * (width - part)
        at_other = (1 - lax.axis_index("dp")) * (width - part)
        moving = lax.dynamic_slice(packed, (0, at_own), (FB, part))
        full = lax.dynamic_update_slice(full, packed, (FB * iy, 0))
        for j in range(1, ROWS):
            moving = ring(moving)
            other = lax.ppermute(moving, "dp", [(0, 1), (1, 0)])
            at = FB * ((iy - j) % ROWS)
            full = lax.dynamic_update_slice(full, moving, (at, at_own))
            full = lax.dynamic_update_slice(full, other, (at, at_other))
        return full
    moving = packed
    for j in range(ROWS):
        if j:
            moving = ring(moving)
        full = lax.dynamic_update_slice(full, moving, (FB * ((iy - j) % ROWS), 0))
    return full


def norm_back(values, scale, gain, grad):
    weighted = grad * gain
    inner = jnp.sum(weighted * values, axis=0, keepdims=True)
    return (
        scale * weighted - values * (scale**3 * inner / D),
        jnp.sum(grad * values * scale, axis=1),
    )


def per_device(
    tokens, segment_ids, slot_table, w_qkv, w_out, w_gate_up, w_down, gain_attn, gain_mlp, cotangent
):
    ix = lax.axis_index("gx")
    iy = lax.axis_index("gy")
    ff = w_down.shape[1]
    odd_row = jnp.sum(jnp.where(slot_table % 2 == 1, slot_table // 2, 0))

    x = to_tokens(tokens, ix, iy)
    w5 = gather_attention_weights(w_qkv, w_out, odd_row, ix, iy)
    gains = lax.all_gather(jnp.stack([gain_attn, gain_mlp]), "gy", axis=1, tiled=True)
    gain_one = gains[0][:, None]
    gain_two = gains[1][:, None]
    seg = lax.ppermute(segment_ids, "gy", [(i, SEQ_MAP[i]) for i in range(ROWS)]).reshape(ROWS, CH)
    w_mlp = gather_mlp_weights(
        jnp.concatenate([w_gate_up[:, 0], w_gate_up[:, 1], w_down], axis=1), iy
    )
    dy = to_tokens(cotangent, ix, iy)

    seg_own = lax.dynamic_index_in_dim(seg, ix, 0, keepdims=False)
    starts = jnp.stack([jnp.sum(seg < s) for s in range(SEGS)]).astype(jnp.int32)
    first = sum(jnp.where(seg_own == s, starts[s], 0) for s in range(SEGS))
    at_own = ix * CH + jnp.arange(CH, dtype=jnp.int32)
    position = (at_own - first).astype(F32)
    frequency = THETA_BASE ** (-2.0 * jnp.arange(HD // 2, dtype=F32) / HD)
    angles = frequency[:, None] * position[None, :]
    cos_a = jnp.cos(angles)
    sin_a = jnp.sin(angles)
    biases = []
    flags = []
    for k in range(ROWS):
        seg_k = lax.dynamic_index_in_dim(seg, ix ^ k, 0, keepdims=False)
        at_k = (ix ^ k) * CH + jnp.arange(CH, dtype=jnp.int32)
        allowed = (seg_k[:, None] == seg_own[None, :]) & (at_k[:, None] <= at_own[None, :])
        biases.append(jnp.where(allowed, 0.0, NEGATIVE).astype(F32))
        flags.append(((ix ^ k) <= ix) & (seg_k[CH - 1] >= seg_own[0]))
    bias = jnp.stack(biases)
    flags = jnp.stack(flags).astype(jnp.int32)

    qs, kv, n1, r1 = call_qkv(x, gain_one, cos_a, sin_a, w5)
    kvs = row_gather(kv)
    o, lse, h, n2, r2 = call_attend(flags, qs, kvs, bias, w5, x, gain_two)

    n2s = row_gather(n2)
    dys = row_gather(dy)
    wg, wu, wd = w_mlp[:, :ff], w_mlp[:, ff : 2 * ff], w_mlp[:, 2 * ff :]
    near = call_mlp(wg, wu, wd, n2s[:2], dys[:2])
    far = call_mlp(wg, wu, wd, n2s[2:], dys[2:])
    blocks = near + far
    dn2 = row_scatter([b[4] for b in blocks])
    mlp = row_scatter([b[3] for b in blocks])
    layer_out = to_features((h + mlp).astype(BF), ix, iy)

    grad_norm, grad_gain_mlp = norm_back(h, r2, gain_two, dn2)
    dh = dy.astype(F32) + grad_norm
    datt = dh.astype(BF)

    dq, dkv0, dkv1, dkv2, dkv3 = call_attend_back(flags, qs, kvs, bias, w5, o, lse, datt, cos_a, sin_a)
    dkv = row_scatter([dkv0, dkv1, dkv2, dkv3])
    half = HD // 2
    dk_a = dkv[:, :half]
    dk_b = dkv[:, half:HD]
    dpg = jnp.concatenate(
        [
            dq,
            (dk_a * cos_a + dk_b * sin_a).astype(BF),
            (dk_b * cos_a - dk_a * sin_a).astype(BF),
            dkv[:, HD:].astype(BF),
        ],
        axis=1,
    )
    dn1 = jnp.einsum("gdc,gct->dt", w5[:, :, :SLOT_W], dpg, preferred_element_type=F32)
    x32 = x.astype(F32)
    grad_in, grad_gain_attn = norm_back(x32, r1, gain_one, dn1)
    input_grad = to_features((dh + grad_in).astype(BF), ix, iy)

    n2_all = jnp.concatenate(n2s, axis=1)
    dy_all = jnp.concatenate(dys, axis=1)
    gate_all = jnp.concatenate([b[1] for b in blocks], axis=1)
    up_all = jnp.concatenate([b[2] for b in blocks], axis=1)
    a_all = jnp.concatenate([b[0] for b in blocks], axis=1)
    g_mlp = jnp.concatenate(
        [nt(n2_all, gate_all).astype(BF), nt(n2_all, up_all).astype(BF), nt(dy_all, a_all).astype(BF)],
        axis=1,
    )
    g_mlp = ring_scatter(lambda at: lax.dynamic_slice(g_mlp, (FB * at, 0), (FB, 3 * ff)), iy)
    g_mlp = dp_sum(g_mlp.astype(BF))

    g_qkv = jnp.einsum("dt,gct->gdc", n1, dpg, preferred_element_type=F32).astype(BF)
    g_out = jnp.einsum("dt,get->gde", datt, o, preferred_element_type=F32).astype(BF)
    g5 = jnp.concatenate([g_qkv, g_out], axis=2)
    packs = [
        jnp.concatenate([g5[k], lax.dynamic_slice(g5[GROUPS - 1], (0, ODD * (ix ^ k)), (D, ODD))], axis=1)
        for k in range(ROWS)
    ]
    g_attn = row_scatter(packs).astype(BF)
    g_attn = ring_scatter(lambda at: lax.dynamic_slice(g_attn, (FB * at, 0), (FB, PACK + ODD)), iy)
    g_attn = dp_sum(g_attn.astype(BF))
    even = g_attn[:, :PACK]
    odd = jnp.zeros((FB, PACK), F32)
    for k, piece in enumerate(row_gather(g_attn[:, PACK:])):
        odd = lax.dynamic_update_slice(odd, piece, (0, ODD * (ix ^ k)))
    odd = jnp.where(ix == odd_row, odd, 0.0)
    grad_qkv = jnp.concatenate([even[:, :SLOT_W], odd[:, :SLOT_W]], axis=1)
    grad_out = jnp.concatenate([even[:, SLOT_W:], odd[:, SLOT_W:]], axis=1)
    grad_gate_up = jnp.stack([g_mlp[:, :ff], g_mlp[:, ff : 2 * ff]], axis=1)
    grad_down = g_mlp[:, 2 * ff :]

    gain_grads = lax.psum(jnp.stack([grad_gain_attn, grad_gain_mlp]), ("dp", "gx", "gy"))
    gain_grads = lax.dynamic_slice(gain_grads, (0, FB * iy), (2, FB))
    return (
        layer_out,
        input_grad,
        grad_qkv,
        grad_out,
        grad_gate_up,
        grad_down,
        gain_grads[0],
        gain_grads[1],
    )


def solution(mesh):
    placed = (
        P("gy", ("dp", "gx")),
        P(("dp", "gy"), None),
        P(),
        P("gy", "gx"),
        P("gy", "gx"),
        P("gy", None, "gx"),
        P("gy", "gx"),
        P("gy"),
        P("gy"),
        P("gy", ("dp", "gx")),
    )
    return jax.shard_map(
        per_device,
        mesh=mesh,
        in_specs=placed,
        out_specs=(
            P("gy", ("dp", "gx")),
            P("gy", ("dp", "gx")),
            P("gy", "gx"),
            P("gy", "gx"),
            P("gy", None, "gx"),
            P("gy", "gx"),
            P("gy"),
            P("gy"),
        ),
        check_vma=False,
    )
```

time: 2270 us -> 682 us (0.30)
  waiting for transfers between devices: 1780 us -> 136 us
  matrix products: 206 us -> 23.1 us
  local copies, waits for them, and re-layouts: 97.1 us -> 218 us
  starting transfers between devices: 1.05 us -> 121 us
  Pallas kernels: 0 us -> 49.4 us
  other arithmetic: 82.1 us -> 51.7 us
    reduce_scatter x4 -> x0, waiting for transfers between devices: 1090 us -> none  [column_sum(): lax.psum_scatter(term_fn(jnp.int32(0), lax.axis_size('gy') * row_count),...]
    all_gather x8 -> x0, waiting for transfers between devices: 520 us -> none  [the longest x2 354 us: fold_block(): lax.all_gather(pieces, 'gy', axis=0, tiled=True)]
    dot_general x40 -> x6, matrix products: 206 us -> 23.1 us  [the longest x3 14 us: nt(): lax.dot_general(a, b, (((1,), (1,)), ((), ())), preferred_element_type=F32)]
    ppermute x0 -> x73, waiting for transfers between devices: none -> 136 us  [the longest x39 69.1 us: swap(): return lax.ppermute(values, 'gx', [(i, i ^ bit) for i in range(ROWS)])]
    unnamed x21 -> x0, waiting for transfers between devices: 123 us -> none
    ppermute x0 -> x73, starting transfers between devices: none -> 121 us  [the longest x39 77.7 us: swap(): return lax.ppermute(values, 'gx', [(i, i ^ bit) for i in range(ROWS)])]
    psum x1 -> x0, waiting for transfers between devices: 49.5 us -> none  [per_device(): lax.psum(grad_gate_up.astype(jnp.bfloat16), 'dp').astype(jnp.float32)]
    pallas_call x0 -> x5, Pallas kernels: none -> 49.4 us  [the longest x2 17.4 us: call_mlp(): pl.pallas_call(mlp_kernel, out_shape=[sds((width, CH), BF), sds((width, C...]
  transfers between devices with their start and end apart: 17 -> 73, of which waited for: 17 -> 26; matrix products, arithmetic and copies ran while one was open for 9% -> 36% of each run, Pallas kernels for 0% -> 5%
where the time goes in v1:
time: 682 us; the launch traced here: 670 us
  local copies, waits for them, and re-layouts  218 us (32%)
  waiting for transfers between devices  136 us (20%)
  starting transfers between devices  121 us (18%)
  blocking collectives  63.2 us (9%)
  other arithmetic  51.7 us (8%)
  Pallas kernels  49.4 us (7%)
  matrix products  23.1 us (3%)
  between operations  8.31 us (1%)
    ppermute x39, starting transfers between devices, swap(): return lax.ppermute(values, 'gx', [(i, i ^ bit) for i in range(ROWS)])  77.7 us
    ppermute x39, waiting for transfers between devices, swap(): return lax.ppermute(values, 'gx', [(i, i ^ bit) for i in range(ROWS)])  69.1 us
    psum x1, blocking collectives, per_device(): lax.psum(jnp.stack([grad_gain_attn, grad_gain_mlp]), ('dp', 'gx', 'gy'))  46.3 us
    unnamed x188, local copies, waits for them, and re-layouts  44.2 us
    ppermute x12, waiting for transfers between devices, ring(): lax.ppermute(values, 'gy', [(i, (i + 1) % ROWS) for i in range(ROWS)])  30.1 us
    ppermute x12, local copies, waits for them, and re-layouts, swap(): return lax.ppermute(values, 'gx', [(i, i ^ bit) for i in range(ROWS)])  27.3 us
    pallas_call x2, Pallas kernels, call_mlp(): pl.pallas_call(mlp_kernel, out_shape=[sds((width, CH), BF), sds((width, C...  17.4 us
    dynamic_update_slice x3, local copies, waits for them, and re-layouts, gather_mlp_weights(): full = lax.dynamic_update_slice(full, moving, (at, at_own))  17.3 us
  transfers between devices with their start and end apart: 73, of which 26 were waited for; matrix products, arithmetic and copies ran while one was open for 36% of the time, Pallas kernels for 5%

profile of v1, /device:TPU:0, one launch (start us, length us, event | category | flops | bytes accessed | tf_op | source)
XLA Modules:
  0.0 670.4 jit_solution(12295138606638996411)
XLA Ops:
  15.2 16.9 %all-gather = f32[4,240,2]{1,2,0:T(2,128)S(1)} all-gather(f32[1,240,2]{1,2,0:T(2,128)S(1)} %maximum_bitcast_fusion.1), channel_id=1, replica_groups=mesh['dp'=2,'gx'=4,'gy'=4] {'gy'}, dimensions={0}, use_global_device_ids=true | all-gather | bytes 9600 | tf_op jit(solution)/shard_map/all_gather | solution.py:417
  65.6 23.5 %collective-permute-start.9 = (bf16[240,640]{1,0:T(8,128)(2,1)S(1)}, bf16[240,640]{1,0:T(8,128)(2,1)S(1)}, u32[]{:S(2)}, u32[]{:S(2)}) collective-permute-start(bf16[240,640]{1,0:T(8,128)(2,1)S(1)} %pad_maximum_fusion.10), channel_id=1, source_target_pairs={{0,8},{4,12},{8,0},{12,4},{1,9},{5,13},{9,1},{13,5},{2,10},{6,14},... | collective-permute-start | bytes 921608 | tf_op jit(solution)/shard_map/ppermute | solution.py:297
  102.6 5.6 collective-permute-done.13
  109.0 3.8 collective-permute-done.15
  119.2 3.9 collective-permute-done.17
  124.4 4.6 collective-permute-done.19
  133.4 8.3 %collective-permute-done.21 = bf16[240,640]{1,0:T(8,128)(2,1)S(1)} collective-permute-done((bf16[240,640]{1,0:T(8,128)(2,1)S(1)}, bf16[240,640]{1,0:T(8,128)(2,1)S(1)}, u32[]{:S(2)}, u32[]{:S(2)}) %collective-permute-start.21) | collective-permute-done | bytes 307232 | tf_op jit(solution)/shard_map/ppermute | solution.py:297
  148.3 6.3 qkv.1
  160.0 9.0 %collective-permute-done.24.kv2 = bf16[5,128,352]{2,1,0:T(8,128)(2,1)} collective-permute-done((bf16[5,128,352]{2,1,0:T(8,128)(2,1)}, bf16[5,128,352]{2,1,0:T(8,128)(2,1)}, u32[]{:S(2)}, u32[]{:S(2)}) %collective-permute-start.24) | collective-permute-done | bytes 450592 | tf_op jit(solution)/shard_map/ppermute | solution.py:297
  180.5 11.7 %attend.1 = (bf16[5,192,352]{2,1,0:T(8,128)(2,1)S(1)}, f32[5,8,352]{2,1,0:T(8,128)S(1)}, f32[960,352]{1,0:T(8,128)S(1)}, bf16[960,352]{1,0:T(8,128)(2,1)S(1)}, f32[1,352]{1,0:T(1,128)S(1)}) custom-call(s32[4]{0:T(128)S(1)} %add_convert_fusion.15.flags, bf16[5,192,352]{2,1,0:T(8,128)(2,1)S(1)} %copy-done.19, bf16[5,128,352]{2,1,0:T(8,128)(2,1)} %get-tuple-element.43.kv0, ...), custom_call_target="tpu_custom_call" | custom-call | tf_op jit(solution)/shard_map/attend/pallas_call | solution.py:245
  197.8 12.9 %collective-permute-start.39 = (bf16[960,352]{0,1:T(8,128)(2,1)}, bf16[960,352]{0,1:T(8,128)(2,1)}, u32[]{:S(2)}, u32[]{:S(2)}) collective-permute-start(bf16[960,352]{0,1:T(8,128)(2,1)} %copy.168), channel_id=1, source_target_pairs={{0,8},{4,12},{8,0},{12,4},{1,9},{5,13},{9,1},{13,5},{2,10},{6,14},... | collective-permute-start | bytes 2027528 | tf_op jit(solution)/shard_map/ppermute | solution.py:297
  214.1 7.9 %collective-permute-done.30 = bf16[240,1024]{1,0:T(8,128)(2,1)S(1)} collective-permute-done((bf16[240,1024]{1,0:T(8,128)(2,1)}, bf16[240,1024]{1,0:T(8,128)(2,1)S(1)}, u32[]{:S(2)}, u32[]{:S(2)}) %collective-permute-start.30) | collective-permute-done | bytes 491552 | tf_op jit(solution)/shard_map/ppermute | solution.py:317
  226.5 10.5 %collective-permute-done.29 = bf16[240,1024]{1,0:T(8,128)(2,1)} collective-permute-done((bf16[240,1024]{1,0:T(8,128)(2,1)}, bf16[240,1024]{1,0:T(8,128)(2,1)}, u32[]{:S(2)}, u32[]{:S(2)}) %collective-permute-start.29) | collective-permute-done | bytes 491552 | tf_op jit(solution)/shard_map/ppermute | solution.py:385
  237.1 6.0 dynamic_update_slice.214
  245.3 5.1 dynamic_update_slice.215
  250.4 5.8 dynamic_update_slice.216
  256.2 5.1 dynamic_update_slice.217
  261.3 5.6 dynamic_update_slice.218
  269.2 5.2 dynamic_update_slice.219
  274.4 4.0 fusion.67
  291.3 8.7 %mlp.3 = (bf16[640,352]{1,0:T(8,128)(2,1)S(1)}, bf16[640,352]{1,0:T(8,128)(2,1)S(1)}, bf16[640,352]{1,0:T(8,128)(2,1)S(1)}, bf16[960,352]{1,0:T(8,128)(2,1)S(1)}...) custom-call(bf16[960,640]{1,0:T(8,128)(2,1)S(1)} %copy-done.7, ...), custom_call_target="tpu_custom_call" | custom-call | tf_op jit(solution)/shard_map/mlp/pallas_call | solution.py:286
  312.5 6.1 concatenate.70
  329.3 8.7 %mlp.2 = (bf16[640,352]{1,0:T(8,128)(2,1)S(1)}, bf16[640,352]{1,0:T(8,128)(2,1)S(1)}, bf16[640,352]{1,0:T(8,128)(2,1)S(1)}, bf16[960,352]{1,0:T(8,128)(2,1)S(1)}...) custom-call(bf16[960,640]{1,0:T(8,128)(2,1)S(1)} %copy-done.8, ...), custom_call_target="tpu_custom_call" | custom-call | tf_op jit(solution)/shard_map/mlp/pallas_call | solution.py:286
  351.4 5.9 concatenate.67
  359.6 4.2 concatenate.68
  363.8 4.4 concatenate.69
  368.2 5.8 convolution_convert_fusion.4
  389.8 5.7 convolution_convert_fusion.3
  395.6 4.1 concatenate.71
  409.8 5.4 collective-permute-done.44
  417.5 5.0 fusion.66
  422.6 14.0 %attend_back.1 = (bf16[5,192,352]{2,1,0:T(8,128)(2,1)S(1)}, f32[5,128,352]{2,1,0:T(8,128)S(1)}, bf16[5,128,352]{2,1,0:T(8,128)(2,1)}, bf16[5,128,352]{2,1,0:T(8,128)(2,1)S(1)}, bf16[5,128,352]{2,1,0:T(8,128)(2,1)S(1)}) custom-call(s32[4]{0:T(128)S(1)} %copy-done.47, bf16[5,192,352]{2,1,0:T(8,128)(2,1)S(1)} %copy-done.20, ...), custom_call_target="tpu_custom_call" | custom-call | tf_op jit(solution)/shard_map/attend_back/pallas_call | solution.py:265
  436.6 7.1 %collective-permute-start.53 = (bf16[5,128,352]{2,1,0:T(8,128)(2,1)S(1)}, bf16[5,128,352]{2,1,0:T(8,128)(2,1)S(1)}, u32[]{:S(2)}, u32[]{:S(2)}) collective-permute-start(bf16[5,128,352]{2,1,0:T(8,128)(2,1)S(1)} %get-tuple-element.62), channel_id=1, source_target_pairs={{0,4},{4,0},{8,12},{12,8},{1,5},{5,1},{9,13},{13,9},{2,6},{6,2},{1... | collective-permute-start | bytes 1351688 | tf_op jit(solution)/shard_map/ppermute | solution.py:297
  447.7 8.6 %collective-permute-start.54 = (bf16[5,128,352]{2,1,0:T(8,128)(2,1)}, bf16[5,128,352]{2,1,0:T(8,128)(2,1)}, u32[]{:S(2)}, u32[]{:S(2)}) collective-permute-start(bf16[5,128,352]{2,1,0:T(8,128)(2,1)} %add_convert_fusion.8), channel_id=1, source_target_pairs={{0,8},{4,12},{8,0},{12,4},{1,9},{5,13},{9,1},{13,5},{2,10},{6,14},... | collective-permute-start | bytes 1351688 | tf_op jit(solution)/shard_map/ppermute | solution.py:297
  461.4 6.3 collective-permute-done.54
  472.8 5.8 copy.206
  478.6 4.7 fusion.11
  489.7 4.4 collective-permute-start.70
  496.6 3.8 collective-permute-start.48
  501.3 16.0 %collective-permute-done.46 = bf16[240,352]{1,0:T(8,128)(2,1)} collective-permute-done((bf16[240,352]{1,0:T(8,128)(2,1)}, bf16[240,352]{1,0:T(8,128)(2,1)}, u32[]{:S(2)}, u32[]{:S(2)}) %collective-permute-start.46) | collective-permute-done | bytes 168992 | tf_op jit(solution)/shard_map/ppermute | solution.py:349
  528.5 11.5 %collective-permute-start.59 = (bf16[960,640]{1,0:T(8,128)(2,1)S(1)}, bf16[960,640]{1,0:T(8,128)(2,1)S(1)}, u32[]{:S(2)}, u32[]{:S(2)}) collective-permute-start(bf16[960,640]{1,0:T(8,128)(2,1)S(1)} %pad_maximum_fusion.3), channel_id=1, source_target_pairs={{0,4},{4,0},{8,12},{12,8},{1,5},{5,1},{9,13},{13,9},{2,6},{6,2},{1... | collective-permute-start | bytes 3686408 | tf_op jit(solution)/shard_map/ppermute | solution.py:297
  544.5 4.4 fusion.7
  550.8 21.8 %collective-permute-done.61 = bf16[960,640]{1,0:T(8,128)(2,1)S(1)} collective-permute-done((bf16[960,640]{1,0:T(8,128)(2,1)S(1)}, bf16[960,640]{1,0:T(8,128)(2,1)S(1)}, u32[]{:S(2)}, u32[]{:S(2)}) %collective-permute-start.61) | collective-permute-done | bytes 1228832 | tf_op jit(solution)/shard_map/ppermute | solution.py:297
  577.2 3.8 collective-permute-start.58
  581.0 46.3 %psum.7 = f32[2,960]{1,0:T(2,128)S(1)} all-reduce(f32[2,960]{1,0:T(2,128)S(1)} %pad_maximum_fusion.13), channel_id=1, replica_groups=mesh['dp'=2,'gx'=4,'gy'=4] {'dp','gx','gy'}, use_global_device_ids=true, to_apply=%region_9.10 | all-reduce | flops 1920 | bytes 15360 | tf_op jit(solution)/shard_map/psum | solution.py:515
  635.2 5.4 collective-permute-done.63
  645.5 5.2 collective-permute-done.64
  652.3 4.3 collective-permute-done.72
  (482 shorter events, 262.8 us)
Async XLA Ops:
  5.8 46.9 %collective-permute-start.6 = (bf16[240,128]{1,0:T(8,128)(2,1)}, bf16[240,128]{1,0:T(8,128)(2,1)S(1)}, u32[]{:S(2)}, u32[]{:S(2)}) collective-permute-start(bf16[240,128]{1,0:T(8,128)(2,1)} %get-tuple-element.176), channel_id=1, source_target_pairs={{0,4},{4,0},{8,12},{12,8},{1,5},{5,1},{9,13},{13,9},{2,6},{6,2},{1... | collective-permute-start | bytes 184328 | tf_op jit(solution)/shard_map/ppermute | solution.py:297
  6.3 48.0 %collective-permute-start.5 = (bf16[240,128]{1,0:T(8,128)(2,1)}, bf16[240,128]{1,0:T(8,128)(2,1)S(1)}, u32[]{:S(2)}, u32[]{:S(2)}) collective-permute-start(bf16[240,128]{1,0:T(8,128)(2,1)} %get-tuple-element.175), channel_id=1, source_target_pairs={{0,4},{4,0},{8,12},{12,8},{1,5},{5,1},{9,13},{13,9},{2,6},{6,2},{1... | collective-permute-start | bytes 184328 | tf_op jit(solution)/shard_map/ppermute | solution.py:297
  7.5 51.9 %collective-permute-start.1 = (bf16[240,352]{1,0:T(8,128)(2,1)}, bf16[240,352]{1,0:T(8,128)(2,1)}, u32[]{:S(2)}, u32[]{:S(2)}) collective-permute-start(bf16[240,352]{1,0:T(8,128)(2,1)} %bitcast.8), channel_id=1, source_target_pairs={{0,0},{1,4},{2,8},{3,12},{4,2},{5,6},{6,10},{7,14},{8,1},{9,5},{10... | collective-permute-start | bytes 506888 | tf_op jit(solution)/shard_map/ppermute | solution.py:340
  11.4 50.6 %collective-permute-start.2 = (bf16[240,352]{1,0:T(8,128)(2,1)}, bf16[240,352]{1,0:T(8,128)(2,1)}, u32[]{:S(2)}, u32[]{:S(2)}) collective-permute-start(bf16[240,352]{1,0:T(8,128)(2,1)} %bitcast.9), channel_id=1, source_target_pairs={{0,4},{1,0},{2,12},{3,8},{4,6},{5,2},{6,14},{7,10},{8,5},{9,1},{10... | collective-permute-start | bytes 506888 | tf_op jit(solution)/shard_map/ppermute | solution.py:340
  14.5 34.8 %collective-permute-start = (s32[1,1408]{1,0:T(1,128)S(1)}, s32[1,1408]{1,0:T(1,128)S(1)}, u32[]{:S(2)}, u32[]{:S(2)}) collective-permute-start(s32[1,1408]{1,0:T(1,128)S(1)} %copy-done.89), channel_id=1, source_target_pairs={{0,0},{1,2},{2,1},{3,3},{4,4},{5,6},{6,5},{7,7},{8,8},{9,10},{10,9... | collective-permute-start | bytes 16904 | tf_op jit(solution)/shard_map/ppermute | solution.py:420
  49.3 16.2 %collective-permute-start.3 = (bf16[240,352]{1,0:T(8,128)(2,1)}, bf16[240,352]{1,0:T(8,128)(2,1)S(1)}, u32[]{:S(2)}, u32[]{:S(2)}) collective-permute-start(bf16[240,352]{1,0:T(8,128)(2,1)} %bitcast.234), channel_id=1, source_target_pairs={{0,8},{1,12},{2,0},{3,4},{4,10},{5,14},{6,2},{7,6},{8,9},{9,13},{1... | collective-permute-start | bytes 506888 | tf_op jit(solution)/shard_map/ppermute | solution.py:340
  57.2 101.2 %collective-permute-start.26 = (bf16[240,1024]{1,0:T(8,128)(2,1)S(1)}, bf16[240,1024]{1,0:T(8,128)(2,1)}, u32[]{:S(2)}, u32[]{:S(2)}) collective-permute-start(bf16[240,1024]{1,0:T(8,128)(2,1)S(1)} %constant_dynamic-slice_fusion.16), channel_id=1, source_target_pairs={{0,1},{1,2},{2,3},{3,0},{4,5},{5,6},{6,7},{7,4},{8,9},{9,10},{10,1... | collective-permute-start | bytes 1474568 | tf_op jit(solution)/shard_map/ppermute | solution.py:317
  59.4 95.3 %collective-permute-start.33 = (bf16[240,352]{1,0:T(8,128)(2,1)}, bf16[240,352]{1,0:T(8,128)(2,1)S(1)}, u32[]{:S(2)}, u32[]{:S(2)}) collective-permute-start(bf16[240,352]{1,0:T(8,128)(2,1)} %bitcast.54), channel_id=1, source_target_pairs={{0,0},{1,4},{2,8},{3,12},{4,2},{5,6},{6,10},{7,14},{8,1},{9,5},{10... | collective-permute-start | bytes 506888 | tf_op jit(solution)/shard_map/ppermute | solution.py:340
  62.0 27.2 %collective-permute-start.8 = (bf16[240,640]{1,0:T(8,128)(2,1)S(1)}, bf16[240,640]{1,0:T(8,128)(2,1)S(1)}, u32[]{:S(2)}, u32[]{:S(2)}) collective-permute-start(bf16[240,640]{1,0:T(8,128)(2,1)S(1)} %pad_maximum_fusion.10), channel_id=1, source_target_pairs={{0,4},{4,0},{8,12},{12,8},{1,5},{5,1},{9,13},{13,9},{2,6},{6,2},{1... | collective-permute-start | bytes 921608 | tf_op jit(solution)/shard_map/ppermute | solution.py:297
  65.5 89.5 %collective-permute-start.34 = (bf16[240,352]{1,0:T(8,128)(2,1)}, bf16[240,352]{1,0:T(8,128)(2,1)S(1)}, u32[]{:S(2)}, u32[]{:S(2)}) collective-permute-start(bf16[240,352]{1,0:T(8,128)(2,1)} %bitcast.55), channel_id=1, source_target_pairs={{0,4},{1,0},{2,12},{3,8},{4,6},{5,2},{6,14},{7,10},{8,5},{9,1},{10... | collective-permute-start | bytes 506888 | tf_op jit(solution)/shard_map/ppermute | solution.py:340
  65.6 28.4 %collective-permute-start.9 = (bf16[240,640]{1,0:T(8,128)(2,1)S(1)}, bf16[240,640]{1,0:T(8,128)(2,1)S(1)}, u32[]{:S(2)}, u32[]{:S(2)}) collective-permute-start(bf16[240,640]{1,0:T(8,128)(2,1)S(1)} %pad_maximum_fusion.10), channel_id=1, source_target_pairs={{0,8},{4,12},{8,0},{12,4},{1,9},{5,13},{9,1},{13,5},{2,10},{6,14},... | collective-permute-start | bytes 921608 | tf_op jit(solution)/shard_map/ppermute | solution.py:297
  129.0 26.0 %collective-permute-start.35 = (bf16[240,352]{1,0:T(8,128)(2,1)}, bf16[240,352]{1,0:T(8,128)(2,1)S(1)}, u32[]{:S(2)}, u32[]{:S(2)}) collective-permute-start(bf16[240,352]{1,0:T(8,128)(2,1)} %bitcast.56), channel_id=1, source_target_pairs={{0,8},{1,12},{2,0},{3,4},{4,10},{5,14},{6,2},{7,6},{8,9},{9,13},{1... | collective-permute-start | bytes 506888 | tf_op jit(solution)/shard_map/ppermute | solution.py:340
  143.3 12.2 %collective-permute-start.36 = (bf16[240,352]{1,0:T(8,128)(2,1)}, bf16[240,352]{1,0:T(8,128)(2,1)S(1)}, u32[]{:S(2)}, u32[]{:S(2)}) collective-permute-start(bf16[240,352]{1,0:T(8,128)(2,1)} %bitcast.57), channel_id=1, source_target_pairs={{0,12},{1,8},{2,4},{3,0},{4,14},{5,10},{6,6},{7,2},{8,13},{9,9},{1... | collective-permute-start | bytes 506888 | tf_op jit(solution)/shard_map/ppermute | solution.py:340
  154.6 14.4 %collective-permute-start.24 = (bf16[5,128,352]{2,1,0:T(8,128)(2,1)}, bf16[5,128,352]{2,1,0:T(8,128)(2,1)}, u32[]{:S(2)}, u32[]{:S(2)}) collective-permute-start(bf16[5,128,352]{2,1,0:T(8,128)(2,1)} %get-tuple-element.43.kv0), channel_id=1, source_target_pairs={{0,8},{4,12},{8,0},{12,4},{1,9},{5,13},{9,1},{13,5},{2,10},{6,14},... | collective-permute-start | bytes 1351688 | tf_op jit(solution)/shard_map/ppermute | solution.py:297
  157.0 53.8 %collective-permute-start.41 = (bf16[960,352]{0,1:T(8,128)(2,1)}, bf16[960,352]{0,1:T(8,128)(2,1)}, u32[]{:S(2)}, u32[]{:S(2)}) collective-permute-start(bf16[960,352]{0,1:T(8,128)(2,1)} %copy.174), channel_id=1, source_target_pairs={{0,8},{4,12},{8,0},{12,4},{1,9},{5,13},{9,1},{13,5},{2,10},{6,14},... | collective-permute-start | bytes 2027528 | tf_op jit(solution)/shard_map/ppermute | solution.py:297
  158.4 52.4 %collective-permute-start.28 = (bf16[240,1024]{1,0:T(8,128)(2,1)}, bf16[240,1024]{1,0:T(8,128)(2,1)}, u32[]{:S(2)}, u32[]{:S(2)}) collective-permute-start(bf16[240,1024]{1,0:T(8,128)(2,1)} %collective-permute-done.26), channel_id=1, source_target_pairs={{0,1},{1,2},{2,3},{3,0},{4,5},{5,6},{6,7},{7,4},{8,9},{9,10},{10,1... | collective-permute-start | bytes 1474568 | tf_op jit(solution)/shard_map/ppermute | solution.py:317
  160.0 18.2 %collective-permute-start.23 = (bf16[5,128,352]{2,1,0:T(8,128)(2,1)}, bf16[5,128,352]{2,1,0:T(8,128)(2,1)}, u32[]{:S(2)}, u32[]{:S(2)}) collective-permute-start(bf16[5,128,352]{2,1,0:T(8,128)(2,1)} %get-tuple-element.43.kv0), channel_id=1, source_target_pairs={{0,4},{4,0},{8,12},{12,8},{1,5},{5,1},{9,13},{13,9},{2,6},{6,2},{1... | collective-permute-start | bytes 1351688 | tf_op jit(solution)/shard_map/ppermute | solution.py:297
  197.8 25.2 %collective-permute-start.39 = (bf16[960,352]{0,1:T(8,128)(2,1)}, bf16[960,352]{0,1:T(8,128)(2,1)}, u32[]{:S(2)}, u32[]{:S(2)}) collective-permute-start(bf16[960,352]{0,1:T(8,128)(2,1)} %copy.168), channel_id=1, source_target_pairs={{0,8},{4,12},{8,0},{12,4},{1,9},{5,13},{9,1},{13,5},{2,10},{6,14},... | collective-permute-start | bytes 2027528 | tf_op jit(solution)/shard_map/ppermute | solution.py:297
  210.8 56.1 %collective-permute-start.42 = (bf16[960,352]{0,1:T(8,128)(2,1)}, bf16[960,352]{0,1:T(8,128)(2,1)}, u32[]{:S(2)}, u32[]{:S(2)}) collective-permute-start(bf16[960,352]{0,1:T(8,128)(2,1)} %collective-permute-done.41), channel_id=1, source_target_pairs={{0,4},{4,0},{8,12},{12,8},{1,5},{5,1},{9,13},{13,9},{2,6},{6,2},{1... | collective-permute-start | bytes 2027528 | tf_op jit(solution)/shard_map/ppermute | solution.py:297
  212.1 14.4 %collective-permute-start.27 = (bf16[240,1024]{1,0:T(8,128)(2,1)}, bf16[240,1024]{1,0:T(8,128)(2,1)}, u32[]{:S(2)}, u32[]{:S(2)}) collective-permute-start(bf16[240,1024]{1,0:T(8,128)(2,1)} %collective-permute-done.26), channel_id=1, source_target_pairs={{0,16},{16,0},{1,17},{17,1},{2,18},{18,2},{3,19},{19,3},{4,20},{20... | collective-permute-start | bytes 1474568 | tf_op jit(solution)/shard_map/ppermute | solution.py:385
  212.1 24.9 %collective-permute-start.29 = (bf16[240,1024]{1,0:T(8,128)(2,1)}, bf16[240,1024]{1,0:T(8,128)(2,1)}, u32[]{:S(2)}, u32[]{:S(2)}) collective-permute-start(bf16[240,1024]{1,0:T(8,128)(2,1)} %collective-permute-done.28), channel_id=1, source_target_pairs={{0,16},{16,0},{1,17},{17,1},{2,18},{18,2},{3,19},{19,3},{4,20},{20... | collective-permute-start | bytes 1474568 | tf_op jit(solution)/shard_map/ppermute | solution.py:385
  222.1 47.2 %collective-permute-start.31 = (bf16[240,1024]{1,0:T(8,128)(2,1)S(1)}, bf16[240,1024]{1,0:T(8,128)(2,1)}, u32[]{:S(2)}, u32[]{:S(2)}) collective-permute-start(bf16[240,1024]{1,0:T(8,128)(2,1)S(1)} %collective-permute-done.30), channel_id=1, source_target_pairs={{0,16},{16,0},{1,17},{17,1},{2,18},{18,2},{3,19},{19,3},{4,20},{20... | collective-permute-start | bytes 1474568 | tf_op jit(solution)/shard_map/ppermute | solution.py:385
  223.1 57.6 %collective-permute-start.40 = (bf16[960,352]{0,1:T(8,128)(2,1)}, bf16[960,352]{0,1:T(8,128)(2,1)}, u32[]{:S(2)}, u32[]{:S(2)}) collective-permute-start(bf16[960,352]{0,1:T(8,128)(2,1)} %collective-permute-done.39), channel_id=1, source_target_pairs={{0,4},{4,0},{8,12},{12,8},{1,5},{5,1},{9,13},{13,9},{2,6},{6,2},{1... | collective-permute-start | bytes 2027528 | tf_op jit(solution)/shard_map/ppermute | solution.py:297
  226.5 83.7 %collective-permute-start.37 = (bf16[960,352]{0,1:T(8,128)(2,1)}, bf16[960,352]{0,1:T(8,128)(2,1)}, u32[]{:S(2)}, u32[]{:S(2)}) collective-permute-start(bf16[960,352]{0,1:T(8,128)(2,1)} %copy.174), channel_id=1, source_target_pairs={{0,4},{4,0},{8,12},{12,8},{1,5},{5,1},{9,13},{13,9},{2,6},{6,2},{1... | collective-permute-start | bytes 2027528 | tf_op jit(solution)/shard_map/ppermute | solution.py:297
  237.1 82.8 %collective-permute-start.32 = (bf16[960,352]{0,1:T(8,128)(2,1)}, bf16[960,352]{0,1:T(8,128)(2,1)}, u32[]{:S(2)}, u32[]{:S(2)}) collective-permute-start(bf16[960,352]{0,1:T(8,128)(2,1)} %copy.168), channel_id=1, source_target_pairs={{0,4},{4,0},{8,12},{12,8},{1,5},{5,1},{9,13},{13,9},{2,6},{6,2},{1... | collective-permute-start | bytes 2027528 | tf_op jit(solution)/shard_map/ppermute | solution.py:297
  309.7 64.3 %collective-permute-start.50 = (bf16[960,352]{0,1:T(8,128)(2,1)}, bf16[960,352]{0,1:T(8,128)(2,1)}, u32[]{:S(2)}, u32[]{:S(2)}) collective-permute-start(bf16[960,352]{0,1:T(8,128)(2,1)} %copy.195), channel_id=1, source_target_pairs={{0,4},{4,0},{8,12},{12,8},{1,5},{5,1},{9,13},{13,9},{2,6},{6,2},{1... | collective-permute-start | bytes 2027528 | tf_op jit(solution)/shard_map/ppermute | solution.py:297
  348.6 51.1 %collective-permute-start.49 = (bf16[960,352]{0,1:T(8,128)(2,1)}, bf16[960,352]{0,1:T(8,128)(2,1)}, u32[]{:S(2)}, u32[]{:S(2)}) collective-permute-start(bf16[960,352]{0,1:T(8,128)(2,1)} %copy.193), channel_id=1, source_target_pairs={{0,4},{4,0},{8,12},{12,8},{1,5},{5,1},{9,13},{13,9},{2,6},{6,2},{1... | collective-permute-start | bytes 2027528 | tf_op jit(solution)/shard_map/ppermute | solution.py:297
  350.9 51.1 %collective-permute-start.38 = (bf16[960,352]{0,1:T(8,128)(2,1)}, bf16[960,352]{0,1:T(8,128)(2,1)}, u32[]{:S(2)}, u32[]{:S(2)}) collective-permute-start(bf16[960,352]{0,1:T(8,128)(2,1)} %copy.177), channel_id=1, source_target_pairs={{0,4},{4,0},{8,12},{12,8},{1,5},{5,1},{9,13},{13,9},{2,6},{6,2},{1... | collective-permute-start | bytes 2027528 | tf_op jit(solution)/shard_map/ppermute | solution.py:297
  359.5 21.6 %collective-permute-start.43 = (bf16[960,352]{0,1:T(8,128)(2,1)}, bf16[960,352]{0,1:T(8,128)(2,1)}, u32[]{:S(2)}, u32[]{:S(2)}) collective-permute-start(bf16[960,352]{0,1:T(8,128)(2,1)} %copy.185), channel_id=1, source_target_pairs={{0,4},{4,0},{8,12},{12,8},{1,5},{5,1},{9,13},{13,9},{2,6},{6,2},{1... | collective-permute-start | bytes 2027528 | tf_op jit(solution)/shard_map/ppermute | solution.py:297
  380.9 23.4 %collective-permute-start.51 = (bf16[960,352]{0,1:T(8,128)(2,1)}, bf16[960,352]{0,1:T(8,128)(2,1)}, u32[]{:S(2)}, u32[]{:S(2)}) collective-permute-start(bf16[960,352]{0,1:T(8,128)(2,1)} %copy.197), channel_id=1, source_target_pairs={{0,8},{4,12},{8,0},{12,4},{1,9},{5,13},{9,1},{13,5},{2,10},{6,14},... | collective-permute-start | bytes 2027528 | tf_op jit(solution)/shard_map/ppermute | solution.py:297
  388.1 27.1 %collective-permute-start.44 = (bf16[960,352]{0,1:T(8,128)(2,1)}, bf16[960,352]{0,1:T(8,128)(2,1)}, u32[]{:S(2)}, u32[]{:S(2)}) collective-permute-start(bf16[960,352]{0,1:T(8,128)(2,1)} %copy.187), channel_id=1, source_target_pairs={{0,8},{4,12},{8,0},{12,4},{1,9},{5,13},{9,1},{13,5},{2,10},{6,14},... | collective-permute-start | bytes 2027528 | tf_op jit(solution)/shard_map/ppermute | solution.py:297
  446.5 14.9 %collective-permute-start.52 = (bf16[5,128,352]{2,1,0:T(8,128)(2,1)}, bf16[5,128,352]{2,1,0:T(8,128)(2,1)}, u32[]{:S(2)}, u32[]{:S(2)}) collective-permute-start(bf16[5,128,352]{2,1,0:T(8,128)(2,1)} %get-tuple-element.60), channel_id=1, source_target_pairs={{0,4},{4,0},{8,12},{12,8},{1,5},{5,1},{9,13},{13,9},{2,6},{6,2},{1... | collective-permute-start | bytes 1351688 | tf_op jit(solution)/shard_map/ppermute | solution.py:297
  447.7 20.0 %collective-permute-start.54 = (bf16[5,128,352]{2,1,0:T(8,128)(2,1)}, bf16[5,128,352]{2,1,0:T(8,128)(2,1)}, u32[]{:S(2)}, u32[]{:S(2)}) collective-permute-start(bf16[5,128,352]{2,1,0:T(8,128)(2,1)} %add_convert_fusion.8), channel_id=1, source_target_pairs={{0,8},{4,12},{8,0},{12,4},{1,9},{5,13},{9,1},{13,5},{2,10},{6,14},... | collective-permute-start | bytes 1351688 | tf_op jit(solution)/shard_map/ppermute | solution.py:297
  457.3 29.8 %collective-permute-start.69 = (bf16[240,1920]{1,0:T(8,128)(2,1)}, bf16[240,1920]{1,0:T(8,128)(2,1)}, u32[]{:S(2)}, u32[]{:S(2)}) collective-permute-start(bf16[240,1920]{1,0:T(8,128)(2,1)} %constant_dynamic-slice_fusion.2), channel_id=1, source_target_pairs={{0,1},{1,2},{2,3},{3,0},{4,5},{5,6},{6,7},{7,4},{8,9},{9,10},{10,1... | collective-permute-start | bytes 2764808 | tf_op jit(solution)/shard_map/ppermute | solution.py:317
  485.4 54.6 %collective-permute-start.60 = (bf16[960,640]{1,0:T(8,128)(2,1)}, bf16[960,640]{1,0:T(8,128)(2,1)}, u32[]{:S(2)}, u32[]{:S(2)}) collective-permute-start(bf16[960,640]{1,0:T(8,128)(2,1)} %pad_maximum_fusion.4), channel_id=1, source_target_pairs={{0,4},{4,0},{8,12},{12,8},{1,5},{5,1},{9,13},{13,9},{2,6},{6,2},{1... | collective-permute-start | bytes 3686408 | tf_op jit(solution)/shard_map/ppermute | solution.py:297
  489.7 52.1 %collective-permute-start.70 = (bf16[240,1920]{1,0:T(8,128)(2,1)}, bf16[240,1920]{1,0:T(8,128)(2,1)}, u32[]{:S(2)}, u32[]{:S(2)}) collective-permute-start(bf16[240,1920]{1,0:T(8,128)(2,1)} %add_convert_fusion.4), channel_id=1, source_target_pairs={{0,1},{1,2},{2,3},{3,0},{4,5},{5,6},{6,7},{7,4},{8,9},{9,10},{10,1... | collective-permute-start | bytes 2764808 | tf_op jit(solution)/shard_map/ppermute | solution.py:317
  494.1 23.2 %collective-permute-start.46 = (bf16[240,352]{1,0:T(8,128)(2,1)}, bf16[240,352]{1,0:T(8,128)(2,1)}, u32[]{:S(2)}, u32[]{:S(2)}) collective-permute-start(bf16[240,352]{1,0:T(8,128)(2,1)} %get-tuple-element.159), channel_id=1, source_target_pairs={{0,1},{1,9},{2,5},{3,13},{4,0},{5,8},{6,4},{7,12},{8,3},{9,11},{10... | collective-permute-start | bytes 506888 | tf_op jit(solution)/shard_map/ppermute | solution.py:349
  494.5 24.8 %collective-permute-start.47 = (bf16[240,352]{1,0:T(8,128)(2,1)}, bf16[240,352]{1,0:T(8,128)(2,1)S(1)}, u32[]{:S(2)}, u32[]{:S(2)}) collective-permute-start(bf16[240,352]{1,0:T(8,128)(2,1)} %get-tuple-element.158), channel_id=1, source_target_pairs={{0,2},{1,10},{2,6},{3,14},{4,3},{5,11},{6,7},{7,15},{8,0},{9,8},{1... | collective-permute-start | bytes 506888 | tf_op jit(solution)/shard_map/ppermute | solution.py:349
  496.6 24.7 %collective-permute-start.48 = (bf16[240,352]{1,0:T(8,128)(2,1)}, bf16[240,352]{1,0:T(8,128)(2,1)}, u32[]{:S(2)}, u32[]{:S(2)}) collective-permute-start(bf16[240,352]{1,0:T(8,128)(2,1)} %get-tuple-element.157), channel_id=1, source_target_pairs={{0,3},{1,11},{2,7},{3,15},{4,2},{5,10},{6,6},{7,14},{8,1},{9,9},{1... | collective-permute-start | bytes 506888 | tf_op jit(solution)/shard_map/ppermute | solution.py:349
  528.5 22.3 %collective-permute-start.59 = (bf16[960,640]{1,0:T(8,128)(2,1)S(1)}, bf16[960,640]{1,0:T(8,128)(2,1)S(1)}, u32[]{:S(2)}, u32[]{:S(2)}) collective-permute-start(bf16[960,640]{1,0:T(8,128)(2,1)S(1)} %pad_maximum_fusion.3), channel_id=1, source_target_pairs={{0,4},{4,0},{8,12},{12,8},{1,5},{5,1},{9,13},{13,9},{2,6},{6,2},{1... | collective-permute-start | bytes 3686408 | tf_op jit(solution)/shard_map/ppermute | solution.py:297
  541.7 30.8 %collective-permute-start.61 = (bf16[960,640]{1,0:T(8,128)(2,1)S(1)}, bf16[960,640]{1,0:T(8,128)(2,1)S(1)}, u32[]{:S(2)}, u32[]{:S(2)}) collective-permute-start(bf16[960,640]{1,0:T(8,128)(2,1)S(1)} %add_convert_fusion.1), channel_id=1, source_target_pairs={{0,8},{4,12},{8,0},{12,4},{1,9},{5,13},{9,1},{13,5},{2,10},{6,14},... | collective-permute-start | bytes 3686408 | tf_op jit(solution)/shard_map/ppermute | solution.py:297
  544.4 86.7 %collective-permute-start.71 = (bf16[240,1920]{1,0:T(8,128)(2,1)}, bf16[240,1920]{1,0:T(8,128)(2,1)}, u32[]{:S(2)}, u32[]{:S(2)}) collective-permute-start(bf16[240,1920]{1,0:T(8,128)(2,1)} %add_convert_fusion.3), channel_id=1, source_target_pairs={{0,1},{1,2},{2,3},{3,0},{4,5},{5,6},{6,7},{7,4},{8,9},{9,10},{10,1... | collective-permute-start | bytes 2764808 | tf_op jit(solution)/shard_map/ppermute | solution.py:317
  550.1 27.1 %collective-permute-start.55 = (bf16[240,352]{1,0:T(8,128)(2,1)S(1)}, bf16[240,352]{1,0:T(8,128)(2,1)S(1)}, u32[]{:S(2)}, u32[]{:S(2)}) collective-permute-start(bf16[240,352]{1,0:T(8,128)(2,1)S(1)} %get-tuple-element.156), channel_id=1, source_target_pairs={{0,0},{1,8},{2,4},{3,12},{4,1},{5,9},{6,5},{7,13},{8,2},{9,10},{10... | collective-permute-start | bytes 506888 | tf_op jit(solution)/shard_map/ppermute | solution.py:349
  573.2 57.0 %collective-permute-start.62 = (bf16[240,640]{1,0:T(8,128)(2,1)S(1)}, bf16[240,640]{1,0:T(8,128)(2,1)S(1)}, u32[]{:S(2)}, u32[]{:S(2)}) collective-permute-start(bf16[240,640]{1,0:T(8,128)(2,1)S(1)} %constant_dynamic-slice_fusion.3), channel_id=1, source_target_pairs={{0,1},{1,2},{2,3},{3,0},{4,5},{5,6},{6,7},{7,4},{8,9},{9,10},{10,1... | collective-permute-start | bytes 921608 | tf_op jit(solution)/shard_map/ppermute | solution.py:317
  573.9 55.1 %collective-permute-start.56 = (bf16[240,352]{1,0:T(8,128)(2,1)}, bf16[240,352]{1,0:T(8,128)(2,1)S(1)}, u32[]{:S(2)}, u32[]{:S(2)}) collective-permute-start(bf16[240,352]{1,0:T(8,128)(2,1)} %get-tuple-element.155), channel_id=1, source_target_pairs={{0,1},{1,9},{2,5},{3,13},{4,0},{5,8},{6,4},{7,12},{8,3},{9,11},{10... | collective-permute-start | bytes 506888 | tf_op jit(solution)/shard_map/ppermute | solution.py:349
  573.9 55.3 %collective-permute-start.57 = (bf16[240,352]{1,0:T(8,128)(2,1)}, bf16[240,352]{1,0:T(8,128)(2,1)S(1)}, u32[]{:S(2)}, u32[]{:S(2)}) collective-permute-start(bf16[240,352]{1,0:T(8,128)(2,1)} %get-tuple-element.154), channel_id=1, source_target_pairs={{0,2},{1,10},{2,6},{3,14},{4,3},{5,11},{6,7},{7,15},{8,0},{9,8},{1... | collective-permute-start | bytes 506888 | tf_op jit(solution)/shard_map/ppermute | solution.py:349
  577.2 52.1 %collective-permute-start.58 = (bf16[240,352]{1,0:T(8,128)(2,1)S(1)}, bf16[240,352]{1,0:T(8,128)(2,1)S(1)}, u32[]{:S(2)}, u32[]{:S(2)}) collective-permute-start(bf16[240,352]{1,0:T(8,128)(2,1)S(1)} %get-tuple-element.153), channel_id=1, source_target_pairs={{0,3},{1,11},{2,7},{3,15},{4,2},{5,10},{6,6},{7,14},{8,1},{9,9},{1... | collective-permute-start | bytes 506888 | tf_op jit(solution)/shard_map/ppermute | solution.py:349
  632.8 23.8 %collective-permute-start.72 = (bf16[240,1920]{1,0:T(8,128)(2,1)S(1)}, bf16[240,1920]{1,0:T(8,128)(2,1)}, u32[]{:S(2)}, u32[]{:S(2)}) collective-permute-start(bf16[240,1920]{1,0:T(8,128)(2,1)S(1)} %add_convert_fusion.2), channel_id=1, source_target_pairs={{0,16},{16,0},{1,17},{17,1},{2,18},{18,2},{3,19},{19,3},{4,20},{20... | collective-permute-start | bytes 2764808 | tf_op jit(solution)/shard_map/ppermute | solution.py:331
  (116 other events, 804.5 us)
